TPU v7x, 32 devices: a whole 2x2x4 slice. The times are simulated.
32 devices in a mesh: aux: 16 (over z, y, core), occ: 2 (over x).
Axes of the slice: x: 2, y: 2, z: 4, core: 2. Of those that a mesh axis runs over, the one named last changes fastest.
Arguments:
- integrals: bfloat16 [128, 21, 512, 512], P('aux', None, 'occ'), may hold values from -0.40234375 to 0.40234375
- orbitals: bfloat16 [3072, 384], replicated, may hold values from -0.109375 to 0.109375
Outputs:
- k_tiles: float32 [512, 21, 512], P('aux', None, 'occ')
All inputs are finite; a program needn't handle non-finite values.
Results may differ from a plain program's by a relative error of at most 0.0017.
Values may be sent and summed in bfloat16 or wider, within the bound.
A program may use at most 192 MiB of HBM per device.

v0:
```python
import jax
import jax.numpy as jnp
from jax import lax
from jax.sharding import PartitionSpec as P

NB = 6


def first_tile(row_index, block_count):
    return row_index * block_count - row_index * (row_index - 1) // 2


def body(integrals, orbitals):
    occ_parts = lax.axis_size("occ")
    my_index = lax.axis_index("occ")
    slab_count = integrals.shape[0]
    row_width = integrals.shape[2]
    tile_size = integrals.shape[3]
    occ_count = orbitals.shape[1]
    block_count = NB
    own_terms = []
    for row_index in range(block_count):
        tile_begin = first_tile(row_index, block_count)
        tile_span = block_count - row_index
        coeffs = orbitals[row_index * tile_size :].reshape(tile_span, tile_size, occ_count)
        own_terms.append(
            jnp.einsum(
                "pkrm,kmi->pri",
                integrals[:, tile_begin : tile_begin + tile_span],
                coeffs,
                preferred_element_type=jnp.float32,
            )
        )
    own_coeffs = lax.dynamic_index_in_dim(
        orbitals.reshape(block_count, occ_parts, row_width, occ_count), my_index, 1, keepdims=False
    )
    partial_list = []
    for col_index in range(1, block_count):
        stacked = jnp.stack(
            [
                integrals[:, first_tile(row_index, block_count) + col_index - row_index]
                for row_index in range(col_index)
            ],
            axis=1,
        )
        partial_list.append(
            jnp.einsum(
                "pkrc,kri->pci", stacked, own_coeffs[:col_index], preferred_element_type=jnp.float32
            )
        )
    partials = jnp.stack(partial_list, axis=1).reshape(
        slab_count, block_count - 1, occ_parts, row_width, occ_count
    )
    received = lax.all_to_all(
        partials.astype(jnp.bfloat16), "occ", split_axis=2, concat_axis=2, tiled=True
    ).astype(partials.dtype)
    summed = jnp.sum(received, axis=2)
    lower_terms = [summed[:, position] for position in range(block_count - 1)]
    totals = [own_terms[0]] + [
        own_terms[row_index] + lower_terms[row_index - 1] for row_index in range(1, block_count)
    ]
    half_transform = (
        jnp.stack(totals, axis=1)
        .reshape(slab_count, block_count * row_width, occ_count)
        .astype(jnp.bfloat16)
    )
    gathered = lax.all_gather(half_transform, "occ", axis=1, tiled=True)
    gathered_view = gathered.reshape(slab_count, occ_parts, block_count, row_width, occ_count)
    row_blocks = [
        gathered_view[:, :, row_index].reshape(slab_count, tile_size, occ_count)
        for row_index in range(block_count)
    ]
    column_terms = []
    for row_index in range(block_count):
        picked = row_blocks[row_index]
        column_terms.append(
            jnp.einsum(
                "pri,pci->rc",
                picked,
                half_transform[:, row_index * row_width :],
                preferred_element_type=jnp.float32,
            )
        )
    return lax.psum_scatter(
        jnp.concatenate(column_terms, axis=1).reshape(
            tile_size // lax.axis_size("aux") * lax.axis_size("aux"), -1, row_width
        ),
        "aux",
        scatter_dimension=0,
        tiled=True,
    )


def solution(mesh):
    placed = (P("aux", None, "occ", None), P())
    return jax.shard_map(
        body, mesh=mesh, in_specs=placed, out_specs=P("aux", None, "occ"), check_vma=False
    )
```

profile of v0, /device:TPU:0, one launch (start us, length us, event | category | flops | bytes accessed | tf_op | source)
XLA Modules:
  0.0 830.4 jit_solution(2951720948109165651)
XLA Ops:
  6.5 19.7 %fusion.67 = (bf16[8,1,256,512]{3,2,1,0:T(8,128)(2,1)}, bf16[8,1,256,512]{3,2,1,0:T(8,128)(2,1)}, bf16[8,1,256,512]{3,2,1,0:T(8,128)(2,1)}, bf16[8,1,256,512]{3,...) fusion(bf16[8,21,256,512]{3,2,1,0:T(8,128)(2,1)} %param.2), kind=kLoop, calls=%fused_computation.82 | loop fusion | bytes 58720256 | tf_op jit(solution)/shard_map/slice | solution.py:41
  26.3 4.1 copy.114
  30.3 3.9 copy.115
  34.2 4.2 convert_bitcast_fusion
  38.5 4.6 copy.104
  43.1 3.9 constant_dynamic-update-slice_fusion.5
  47.0 3.9 copy.117
  50.9 3.9 copy.118
  54.8 3.9 copy.119
  58.7 3.9 copy.121
  62.6 3.9 copy.122
  66.6 3.9 copy.123
  70.5 3.9 copy.124
  74.4 3.9 copy.126
  78.3 3.1 constant_dynamic-update-slice_fusion.4
  81.3 3.9 copy.127
  85.2 3.9 copy.128
  89.1 3.9 copy.129
  93.0 3.9 copy.130
  96.9 2.6 pad_maximum_fusion.2
  99.6 4.1 fusion.14
  104.6 4.8 fusion.16
  110.6 4.3 copy-done
  114.9 5.5 fusion.18
  127.3 10.1 %fusion.20 = bf16[8,5,2,256,384]{4,3,2,0,1:T(8,128)(2,1)S(1)} fusion(bf16[8,5,2,256,384]{4,3,2,0,1:T(8,128)(2,1)S(1)} %fusion.18, bf16[8,2,256,5,256]{4,2,1,3,0:T(8,128)(2,1)} %bitcast.308, bf16[6,2,256,384]{3,2,1,0:T(8,128)(2,1)S(1)} %bitcast.292, s32[]{:T(128)S(6)} %select_n.4), kind=kOutput, calls=%fused_computation.25 | convolution fusion | flops 4028104704 | bytes 14614532 | tf_op jit(solution)/shard_map/pkrc,kri->pci/dot_general | solution.py:47
  137.3 6.7 copy.75
  144.0 9.3 %all-to-all-start = ((bf16[8,5,2,256,384]{4,3,0,1,2:T(8,128)(2,1)}), bf16[8,5,2,256,384]{4,3,0,1,2:T(8,128)(2,1)}, u32[]{:S(2)}, u32[]{:S(2)}) async-start(bf16[8,5,2,256,384]{4,3,0,1,2:T(8,128)(2,1)} %copy.75), calls=%async_computation | async-start | bytes 31457280 | tf_op jit(solution)/shard_map/all_to_all | solution.py:54
  157.3 11.0 %bitcast_dynamic-update-slice_fusion.7 = bf16[8,6,256,384]{3,2,0,1:T(8,128)(2,1)} fusion(bf16[8,21,256,512]{3,2,1,0:T(8,128)(2,1)} %param.2, bf16[6,512,384,1]{2,1,0,3:T(8,128)(2,1)S(1)} %bitcast.293), kind=kOutput, calls=%fused_computation.59 | convolution fusion | flops 4832624640 | bytes 47972352 | tf_op jit(solution)/shard_map/pkrm,kmi->pri/dot_general | solution.py:27
  168.3 157.5 %all-to-all-done = bf16[8,5,2,256,384]{4,3,0,1,2:T(8,128)(2,1)} async-done(((bf16[8,5,2,256,384]{4,3,0,1,2:T(8,128)(2,1)}), bf16[8,5,2,256,384]{4,3,0,1,2:T(8,128)(2,1)}, u32[]{:S(2)}, u32[]{:S(2)}) %all-to-all-start) | async-done | bytes 15728672 | tf_op jit(solution)/shard_map/all_to_all | solution.py:54
  325.9 22.0 %convert_reduce_fusion = f32[8,5,256,384]{3,2,0,1:T(8,128)} fusion(bf16[8,5,2,256,384]{4,3,0,1,2:T(8,128)(2,1)} %all-to-all-done), kind=kLoop, calls=%fused_computation | loop fusion | flops 11796480 | bytes 31457280 | tf_op jit(solution)/shard_map/reduce_sum | solution.py:57
  347.9 12.3 %bitcast_dynamic-update-slice_fusion.6 = bf16[8,6,256,384]{3,2,0,1:T(8,128)(2,1)} fusion(bf16[8,6,256,384]{3,2,0,1:T(8,128)(2,1)} %bitcast_dynamic-update-slice_fusion.7, f32[8,5,256,384]{3,2,0,1:T(8,128)} %convert_reduce_fusion, bf16[8,21,256,512]{3,2,1,0:T(8,128)(2,1)} %param.2, bf16[5,512,384,1]{2,1,0,3:T(8,128)(2,1)} %bitcast.304), kind=kOutput, calls=%fused_computation.58 | convolution fusion | flops 4028104704 | bytes 50724864 | tf_op jit(solution)/shard_map/pkrm,kmi->pri/dot_general | solution.py:27
  360.2 9.1 %bitcast_dynamic-update-slice_fusion.5 = bf16[8,6,256,384]{3,2,0,1:T(8,128)(2,1)} fusion(bf16[8,6,256,384]{3,2,0,1:T(8,128)(2,1)} %bitcast_dynamic-update-slice_fusion.6, f32[8,5,256,384]{3,2,0,1:T(8,128)S(1)} %copy-done.1, bf16[8,21,256,512]{3,2,1,0:T(8,128)(2,1)} %param.2, bf16[4,512,384,1]{2,1,0,3:T(8,128)(2,1)S(1)} %bitcast.305), kind=kOutput, calls=%fused_computation.57 | convolution fusion | flops 3222798336 | bytes 50331648 | tf_op jit(solution)/shard_map/pkrm,kmi->pri/dot_general | solution.py:27
  369.4 7.8 bitcast_dynamic-update-slice_fusion.4
  377.2 5.8 bitcast_dynamic-update-slice_fusion.3
  383.0 4.0 bitcast_dynamic-update-slice_fusion.2
  387.0 9.0 %copy.77 = bf16[8,6,256,384]{3,2,1,0:T(8,128)(2,1)} copy(bf16[8,6,256,384]{3,2,0,1:T(8,128)(2,1)} %bitcast_dynamic-update-slice_fusion.2) | data formatting | bytes 18874368 | tf_op jit(solution)/shard_map/stack | solution.py:63
  396.0 223.8 %all-gather.2.cloned.1.call-done = bf16[8,3072,384]{2,1,0:T(8,128)(2,1)} async-done(((bf16[8,1536,384]{2,1,0:T(8,128)(2,1)}), bf16[8,3072,384]{2,1,0:T(8,128)(2,1)}) %all-gather.2.cloned.1.call-update) | async-done | bytes 18874384 | tf_op jit(solution)/shard_map/all_gather | solution.py:67
  619.8 13.4 %fusion.68 = (bf16[8,2,1,256,384]{4,3,2,1,0:T(8,128)(2,1)S(1)}, bf16[8,2,1,256,384]{4,3,2,1,0:T(8,128)(2,1)}, bf16[8,2,1,256,384]{4,3,2,1,0:T(8,128)(2,1)}, bf16...) fusion(bf16[8,2,6,256,384]{4,3,2,1,0:T(8,128)(2,1)} %bitcast.287), kind=kLoop, calls=%fused_computation.83 | loop fusion | bytes 37748736 | tf_op jit(solution)/shard_map/slice | solution.py:70
  634.2 8.1 fusion.12
  642.3 5.9 fusion.9
  648.2 4.9 bitcast_dynamic-update-slice_fusion
  653.1 3.8 bitcast_dynamic-update-slice_fusion.1
  656.9 2.9 fusion.51
  659.8 1.9 fusion.57
  661.7 12.1 %copy.86 = f32[512,5376]{0,1:T(8,128)} copy(f32[512,5376]{1,0:T(8,128)} %fusion.57) | data formatting | bytes 22020096 | tf_op jit(solution)/shard_map/concatenate | solution.py:85
  673.8 12.3 %copy.87 = f32[512,21,256]{2,1,0:T(8,128)} copy(f32[512,21,256]{0,2,1:T(8,128)} %bitcast.277) | data formatting | bytes 22020096 | tf_op jit(solution)/shard_map/reshape | solution.py:85
  686.2 134.8 %reduce-scatter.2.cloned.1.call-done = f32[32,21,256]{2,1,0:T(8,128)} async-done(((f32[512,21,256]{2,1,0:T(8,128)}), f32[32,21,256]{2,1,0:T(8,128)}) %reduce-scatter.2.cloned.1.call-update) | async-done | bytes 688144 | tf_op jit(solution)/shard_map/reduce_scatter | solution.py:84
  820.9 2.2 copy.88
  (60 shorter events, 13.8 us)
Async XLA Ops:
  26.2 8.0 copy-start.2
  99.6 4.1 copy-start.7
  99.6 4.1 copy-start.8
  99.6 4.1 copy-start.9
  104.5 4.9 copy-start.10
  104.5 4.9 copy-start.11
  104.5 4.9 copy-start.12
  104.5 4.9 copy-start.13
  109.4 5.5 copy-start
  114.9 5.5 copy-start.5
  120.5 2.3 copy-start.6
  120.5 3.8 copy-start.3
  122.8 3.0 copy-start.4
  144.0 181.9 %all-to-all-start = ((bf16[8,5,2,256,384]{4,3,0,1,2:T(8,128)(2,1)}), bf16[8,5,2,256,384]{4,3,0,1,2:T(8,128)(2,1)}, u32[]{:S(2)}, u32[]{:S(2)}) async-start(bf16[8,5,2,256,384]{4,3,0,1,2:T(8,128)(2,1)} %copy.75), calls=%async_computation | async-start | bytes 31457280 | tf_op jit(solution)/shard_map/all_to_all | solution.py:54
  153.4 466.4 %all-gather.2.cloned.1.call-start = ((), (), s32[]{:S(2)}) async-start(), calls=%async_computation.2 | async-start | bytes 28311552 | tf_op jit(solution)/shard_map/all_gather | solution.py:67
  347.9 12.3 %copy-start.1 = (f32[8,5,256,384]{3,2,0,1:T(8,128)S(1)}, f32[8,5,256,384]{3,2,0,1:T(8,128)}, u32[]{:S(2)}) copy-start(f32[8,5,256,384]{3,2,0,1:T(8,128)} %convert_reduce_fusion) | copy-start | bytes 47185924
  347.9 12.3 %copy-start.18 = (bf16[2048,384]{1,0:T(8,128)(2,1)S(1)}, bf16[2048,384]{1,0:T(8,128)(2,1)}, u32[]{:S(2)}) copy-start(bf16[2048,384]{1,0:T(8,128)(2,1)} %slice.183) | copy-start | bytes 4718596
  369.4 7.8 copy-start.19
  396.0 237.2 %slice-start = ((s8[9437184]{0:T(1024)(128)(4,1)}), s8[1048576]{0:T(1024)(128)(4,1)S(1)}, s32[]{:S(2)}) async-start(s8[9437184]{0:T(1024)(128)(4,1)} %bitcast.279), calls=%async_computation.4 | async-start | bytes 2097152
  396.0 425.0 %reduce-scatter.2.cloned.1.call-start = ((), (), s32[]{:S(2)}) async-start(), calls=%async_computation.3 | async-start | bytes 13369344 | tf_op jit(solution)/shard_map/reduce_scatter | solution.py:84
  619.8 13.4 %slice-start.1 = ((s8[9437184]{0:T(1024)(128)(4,1)}), s8[4194304]{0:T(1024)(128)(4,1)S(1)}, s32[]{:S(2)}) async-start(s8[9437184]{0:T(1024)(128)(4,1)} %bitcast.279), calls=%async_computation.5 | async-start | bytes 8388608
  619.8 14.4 %slice-start.2 = ((s8[9437184]{0:T(1024)(128)(4,1)}), s8[4194304]{0:T(1024)(128)(4,1)S(1)}, s32[]{:S(2)}) async-start(s8[9437184]{0:T(1024)(128)(4,1)} %bitcast.279), calls=%async_computation.6 | async-start | bytes 8388608
  634.2 8.1 copy-start.17
  642.3 5.9 copy-start.16
  648.2 4.9 copy-start.15
  653.1 3.8 copy-start.14
Sparse Core Ops, SparseCore 0:
  396.1 223.6 all-gather.1
  686.3 134.5 reduce-scatter.1
where the time goes:
time: 840 us; the launch traced here: 830 us
  waiting for transfers between devices  516 us (61%)
  local copies, waits for them, and re-layouts  158 us (19%)
  matrix products  106 us (13%)
  other arithmetic  26.5 us (3%)
  between operations  14 us (2%)
  starting transfers between devices  9.43 us (1%)
    all_gather x1, waiting for transfers between devices, body(): gathered = lax.all_gather(half_transform, 'occ', axis=1, tiled=True)  224 us
    all_to_all x1, waiting for transfers between devices, body(): lax.all_to_all(partials.astype(jnp.bfloat16), 'occ', split_axis=2, concat...  158 us
    reduce_scatter x1, waiting for transfers between devices, body(): lax.psum_scatter(jnp.concatenate(column_terms, axis=1).reshape(tile_size...  135 us
    unnamed x65, local copies, waits for them, and re-layouts  72.5 us
    dot_general x6, matrix products, body(): jnp.einsum('pkrm,kmi->pri', integrals[:, tile_begin:tile_begin + tile_spa...  50.1 us
    dot_general x5, matrix products, body(): jnp.einsum('pkrc,kri->pci', stacked, own_coeffs[:col_index], preferred_el...  28.8 us
    dot_general x6, matrix products, body(): jnp.einsum('pri,pci->rc', picked, half_transform[:, row_index * row_width...  27.5 us
    reduce_sum x1, other arithmetic, body(): summed = jnp.sum(received, axis=2)  22 us
  transfers between devices with their start and end apart: 3, of which 3 were waited for; matrix products, arithmetic and copies ran while one was open for 2% of the time, Pallas kernels for 0%

commit v1 on v0

--- a/solution.py
+++ b/solution.py
@@ -1,6 +1,10 @@
+import functools
+
 import jax
 import jax.numpy as jnp
 from jax import lax
+from jax.experimental import pallas as pl
+from jax.experimental.pallas import tpu as pltpu
 from jax.sharding import PartitionSpec as P
 
 NB = 6
@@ -10,7 +14,7 @@
     return row_index * block_count - row_index * (row_index - 1) // 2
 
 
-def body(integrals, orbitals):
+def column_body(integrals, orbitals):
     occ_parts = lax.axis_size("occ")
     my_index = lax.axis_index("occ")
     slab_count = integrals.shape[0]
@@ -90,6 +94,196 @@
         tiled=True,
     )
 
+VMEM_LIMIT = 40 * 1024 * 1024
+
+
+def tile_at(row_index, col_index):
+    low, high = min(row_index, col_index), max(row_index, col_index)
+    return first_tile(low, NB) + high - low
+
+
+def half_kernel(block, owned, where, coeffs, *refs):
+    tiles, refs = refs[:NB], refs[NB:]
+    row_width, tile_size = tiles[0].shape[2:]
+    me = where[0]
+    mine = pl.ds(pl.multiple_of(me * row_width, row_width), row_width)
+    own = sum(
+        lax.dot_general(
+            coeffs[:, at * tile_size : (at + 1) * tile_size],
+            tiles[at][0, 0],
+            (((1,), (1,)), ((), ())),
+            preferred_element_type=jnp.float32,
+        )
+        for at in range(block, NB)
+    )
+    lower = None
+    for at in range(block):
+        rows = pl.ds(pl.multiple_of(at * tile_size + me * row_width, row_width), row_width)
+        term = jnp.dot(coeffs[:, rows], tiles[at][0, 0], preferred_element_type=jnp.float32)
+        lower = term if lower is None else lower + term
+    if not owned:
+        out, total = refs
+        if block == 0:
+            out[0] = own.astype(out.dtype)
+            return
+        total[...] = lower
+        total[:, mine] += own
+        out[0] = total[...].astype(out.dtype)
+        return
+    received, out, total = refs
+    if block == 0:
+        other = pl.ds(pl.multiple_of((1 - me) * row_width, row_width), row_width)
+        total[:, mine] = own
+        total[:, other] = received[0].astype(jnp.float32)
+    else:
+        total[...] = lower + received[0].astype(jnp.float32)
+        total[:, mine] += own
+    out[...] = total[...].T.astype(out.dtype)
+
+
+def half_call(block, owned, where, coeffs, integrals, received=None):
+    slab_count, _, row_width, tile_size = integrals.shape
+    occ_count = coeffs.shape[0]
+    count = slab_count // 2
+    width = row_width if block == 0 else tile_size
+    at = 1 if owned else 2
+
+    def tile_spec(tile):
+        return pl.BlockSpec(
+            (1, 1, row_width, tile_size), lambda p, where: (where[at] + p, tile, 0, 0)
+        )
+
+    moved = pl.BlockSpec((1, occ_count, width), lambda p, where: (p, 0, 0))
+    in_specs = [pl.BlockSpec(coeffs.shape, lambda p, where: (0, 0))]
+    in_specs += [tile_spec(tile_at(block, other)) for other in range(NB)]
+    args = [coeffs] + [integrals] * NB
+    if owned:
+        in_specs.append(moved)
+        args.append(received)
+        out_shape = jax.ShapeDtypeStruct((tile_size, count * occ_count), jnp.bfloat16)
+        out_spec = pl.BlockSpec((tile_size, occ_count), lambda p, where: (0, p))
+    else:
+        out_shape = jax.ShapeDtypeStruct((count, occ_count, width), jnp.bfloat16)
+        out_spec = moved
+    return pl.pallas_call(
+        functools.partial(half_kernel, block, owned),
+        out_shape=out_shape,
+        grid_spec=pltpu.PrefetchScalarGridSpec(
+            num_scalar_prefetch=1,
+            grid=(count,),
+            in_specs=in_specs,
+            out_specs=out_spec,
+            scratch_shapes=[pltpu.VMEM((occ_count, tile_size), jnp.float32)],
+        ),
+        compiler_params=pltpu.CompilerParams(vmem_limit_bytes=VMEM_LIMIT),
+        cost_estimate=pl.CostEstimate(
+            flops=2 * count * NB * row_width * tile_size * occ_count,
+            bytes_accessed=count * NB * row_width * tile_size * 2 + coeffs.size * 2,
+            transcendentals=0,
+        ),
+        name=f"half_{'own' if owned else 'send'}_{block}",
+    )(where, *args)
+
+
+def bit_reverse(value, bits):
+    return sum(((value >> bit) & 1) << (bits - 1 - bit) for bit in range(bits))
+
+
+def tile_kernel(bits, where, *refs):
+    halves, (keep, send, total) = refs[:-3], refs[-3:]
+    parts = 2**bits
+    rows, cols = keep.shape[3:]
+    for at, left in enumerate(halves):
+        total[...] = lax.dot_general(
+            left[...],
+            halves[-1][...],
+            (((1,), (1,)), ((), ())),
+            preferred_element_type=jnp.float32,
+        )
+        for place in range(parts):
+            out = keep if place < parts // 2 else send
+            owner = lax.bitwise_xor(where[3], jnp.int32(bit_reverse(place, bits)))
+            picked = pl.ds(pl.multiple_of(owner * rows, rows), rows)
+            for side in range(2):
+                half = lax.bitwise_xor(where[0], jnp.int32(side))
+                out[place % (parts // 2), side, at] = total[
+                    picked, pl.ds(pl.multiple_of(half * cols, cols), cols)
+                ]
+
+
+def tile_call(bits, where, halves):
+    parts = 2**bits
+    tile_size, depth = halves[0].shape
+    count = len(halves)
+    out = jax.ShapeDtypeStruct(
+        (parts // 2, 2, count, tile_size // parts, tile_size // 2), jnp.float32
+    )
+    return pl.pallas_call(
+        functools.partial(tile_kernel, bits),
+        out_shape=[out, out],
+        in_specs=[pl.BlockSpec(memory_space=pltpu.SMEM)]
+        + [pl.BlockSpec(memory_space=pltpu.VMEM)] * count,
+        out_specs=[pl.BlockSpec(memory_space=pltpu.VMEM)] * 2,
+        scratch_shapes=[pltpu.VMEM((tile_size, tile_size), jnp.float32)],
+        compiler_params=pltpu.CompilerParams(vmem_limit_bytes=VMEM_LIMIT),
+        cost_estimate=pl.CostEstimate(
+            flops=2 * count * tile_size * tile_size * depth,
+            bytes_accessed=count * (tile_size * depth * 2 + tile_size * tile_size * 4),
+            transcendentals=0,
+        ),
+        name=f"tiles_{count - 1}",
+    )(where, *halves)
+
+
+def slab_body(integrals, orbitals):
+    parts = lax.axis_size("aux")
+    bits = parts.bit_length() - 1
+    me = lax.axis_index("occ")
+    count = integrals.shape[0] // 2
+    where = jnp.stack(
+        [me, me * count, (1 - me) * count, lax.axis_index("aux")]
+    ).astype(jnp.int32)
+    coeffs = orbitals.T
+    swap = [(0, 1), (1, 0)]
+    received = []
+    for block in range(NB):
+        sent = half_call(block, False, where, coeffs, integrals)
+        if block >= 2:
+            sent, received[-2] = lax.optimization_barrier((sent, received[-2]))
+        received.append(lax.ppermute(sent, "occ", swap))
+    halves, columns = [], []
+    for block in range(NB):
+        halves.append(half_call(block, True, where, coeffs, integrals, received[block]))
+        keep, send = tile_call(bits, where, halves)
+        for step in range(bits):
+            pairs = [(at, at ^ (1 << step)) for at in range(parts)]
+            came = lax.ppermute(send, "aux", pairs)
+            if step < bits - 1:
+                middle = keep.shape[0] // 2
+                send = keep[middle:] + came[middle:]
+                keep = keep[:middle] + came[:middle]
+            else:
+                send = keep[:, 1] + came[:, 1]
+                keep = keep[:, 0] + came[:, 0]
+        columns.append((keep + lax.ppermute(send, "occ", swap))[0])
+    order = [columns[high][low] for low in range(NB) for high in range(low, NB)]
+    return jnp.stack(order, axis=1)
+
+
+def body(integrals, orbitals):
+    parts = lax.axis_size("aux")
+    slab_count, _, row_width, tile_size = integrals.shape
+    fits = (
+        lax.axis_size("occ") == 2
+        and slab_count % 2 == 0
+        and parts >= 2
+        and parts & (parts - 1) == 0
+        and tile_size % (8 * parts) == 0
+        and row_width % 128 == 0
+        and orbitals.shape[1] % 128 == 0
+    )
+    return (slab_body if fits else column_body)(integrals, orbitals)
+
 
 def solution(mesh):
     placed = (P("aux", None, "occ", None), P())

time: 840 us -> 389 us (0.46)
  waiting for transfers between devices: 516 us -> 203 us
  local copies, waits for them, and re-layouts: 158 us -> 5.83 us
  Pallas kernels: 0 us -> 112 us
  matrix products: 106 us -> 0 us
  starting transfers between devices: 9.43 us -> 51 us
  between operations: 14 us -> 0.44 us
  other arithmetic: 26.5 us -> 15.4 us
    all_gather x1 -> x0, waiting for transfers between devices: 224 us -> none  [body(): gathered = lax.all_gather(half_transform, 'occ', axis=1, tiled=True)]
    ppermute x0 -> x36, waiting for transfers between devices: none -> 203 us  [the longest x24 115 us: slab_body(): came = lax.ppermute(send, 'aux', pairs)]
    all_to_all x1 -> x0, waiting for transfers between devices: 158 us -> none  [body(): lax.all_to_all(partials.astype(jnp.bfloat16), 'occ', split_axis=2, concat...]
    reduce_scatter x1 -> x0, waiting for transfers between devices: 135 us -> none  [body(): lax.psum_scatter(jnp.concatenate(column_terms, axis=1).reshape(tile_size...]
    pallas_call x0 -> x18, Pallas kernels: none -> 112 us  [the longest x12 82.9 us: half_call(): pl.pallas_call(functools.partial(half_kernel, block, owned), out_shape=ou...]
    dot_general x17 -> x0, matrix products: 106 us -> none  [the longest x6 50.1 us: body(): jnp.einsum('pkrm,kmi->pri', integrals[:, tile_begin:tile_begin + tile_spa...]
    unnamed x65 -> x46, local copies, waits for them, and re-layouts: 72.5 us -> 5.21 us
    ppermute x0 -> x36, starting transfers between devices: none -> 51 us  [the longest x24 30.5 us: slab_body(): came = lax.ppermute(send, 'aux', pairs)]
  transfers between devices with their start and end apart: 3 -> 36, of which waited for: 3 -> 20; matrix products, arithmetic and copies ran while one was open for 2% -> 4% of each run, Pallas kernels for 0% -> 27%
where the time goes in v1:
time: 389 us; the launch traced here: 387 us
  waiting for transfers between devices  203 us (52%)
  Pallas kernels  112 us (29%)
  starting transfers between devices  51 us (13%)
  other arithmetic  15.4 us (4%)
  local copies, waits for them, and re-layouts  5.83 us (1%)
    ppermute x24, waiting for transfers between devices, slab_body(): came = lax.ppermute(send, 'aux', pairs)  115 us
    pallas_call x12, Pallas kernels, half_call(): pl.pallas_call(functools.partial(half_kernel, block, owned), out_shape=ou...  82.9 us
    ppermute x6, waiting for transfers between devices, slab_body(): received.append(lax.ppermute(sent, 'occ', swap))  77 us
    ppermute x24, starting transfers between devices, slab_body(): came = lax.ppermute(send, 'aux', pairs)  30.5 us
    pallas_call x6, Pallas kernels, tile_call(): pl.pallas_call(functools.partial(tile_kernel, bits), out_shape=[out, out]...  29.1 us
    add x18, other arithmetic, slab_body(): keep = keep[:middle] + came[:middle]  15.1 us
    ppermute x6, starting transfers between devices, slab_body(): received.append(lax.ppermute(sent, 'occ', swap))  11.2 us
    ppermute x6, waiting for transfers between devices, slab_body(): columns.append((keep + lax.ppermute(send, 'occ', swap))[0])  10.5 us
  transfers between devices with their start and end apart: 36, of which 20 were waited for; matrix products, arithmetic and copies ran while one was open for 4% of the time, Pallas kernels for 27%

profile of v1, /device:TPU:0, one launch (start us, length us, event | category | flops | bytes accessed | tf_op | source)
XLA Modules:
  0.0 387.4 jit_solution(771861355446983791)
XLA Ops:
  0.0 2.8 copy.3
  2.9 6.7 %half_send_0.1 = bf16[4,384,256]{2,1,0:T(8,128)(2,1)} custom-call(s32[4]{0:T(128)S(1)} %pad_add_fusion.where, bf16[384,3072]{1,0:T(8,128)(2,1)S(1)} %bitcast.129, bf16[8,21,256,512]{3,2,1,0:T(8,128)(2,1)} %refs_5_.23, bf16[8,21,256,512]{3,2,1,0:T(8,128)(2,1)} %refs_5_.23, bf16[8,21,256,512]{3,2,1,0:T(8,128)(2,1)} %refs_5_.23, ...), custom_call_target="tpu_custom_call" | custom-call | flops 2415919104 | bytes 8650752 | tf_op jit(solution)/shard_map/half_send_0/pallas_call | solution.py:168
  9.6 2.9 collective-permute-start
  12.5 7.0 %half_send_1.1 = bf16[4,384,512]{2,1,0:T(8,128)(2,1)} custom-call(s32[4]{0:T(128)S(1)} %pad_add_fusion.where, bf16[384,3072]{1,0:T(8,128)(2,1)S(1)} %bitcast.130, bf16[8,21,256,512]{3,2,1,0:T(8,128)(2,1)} %refs_5_.23, bf16[8,21,256,512]{3,2,1,0:T(8,128)(2,1)} %refs_5_.23, bf16[8,21,256,512]{3,2,1,0:T(8,128)(2,1)} %refs_5_.23, ...), custom_call_target="tpu_custom_call" | custom-call | flops 2415919104 | bytes 8650752 | tf_op jit(solution)/shard_map/half_send_1/pallas_call | solution.py:168
  19.6 7.0 %half_send_2.1 = bf16[4,384,512]{2,1,0:T(8,128)(2,1)} custom-call(s32[4]{0:T(128)S(1)} %pad_add_fusion.where, bf16[384,3072]{1,0:T(8,128)(2,1)S(1)} %bitcast.131, bf16[8,21,256,512]{3,2,1,0:T(8,128)(2,1)} %refs_5_.23, bf16[8,21,256,512]{3,2,1,0:T(8,128)(2,1)} %refs_5_.23, bf16[8,21,256,512]{3,2,1,0:T(8,128)(2,1)} %refs_5_.23, ...), custom_call_target="tpu_custom_call" | custom-call | flops 2415919104 | bytes 8650752 | tf_op jit(solution)/shard_map/half_send_2/pallas_call | solution.py:168
  26.6 4.6 %collective-permute-done.refs_6_ = bf16[4,384,256]{2,1,0:T(8,128)(2,1)} collective-permute-done((bf16[4,384,256]{2,1,0:T(8,128)(2,1)}, bf16[4,384,256]{2,1,0:T(8,128)(2,1)}, u32[]{:S(2)}, u32[]{:S(2)}) %collective-permute-start) | collective-permute-done | bytes 786464 | tf_op jit(solution)/shard_map/ppermute | solution.py:253
  31.2 2.1 collective-permute-start.12
  33.3 6.7 %half_own_0.1.refs_0_ = bf16[512,1536]{1,0:T(8,128)(2,1)S(1)} custom-call(s32[4]{0:T(128)S(1)} %pad_add_fusion.where, bf16[384,3072]{1,0:T(8,128)(2,1)S(1)} %bitcast.132, bf16[8,21,256,512]{3,2,1,0:T(8,128)(2,1)} %refs_5_.23, bf16[8,21,256,512]{3,2,1,0:T(8,128)(2,1)} %refs_5_.23, bf16[8,21,256,512]{3,2,1,0:T(8,128)(2,1)} %refs_5_.23, ...), custom_call_target="tpu_custom_call" | custom-call | flops 2415919104 | bytes 8650752 | tf_op jit(solution)/shard_map/half_own_0/pallas_call | solution.py:168
  41.7 6.9 %half_send_3.1 = bf16[4,384,512]{2,1,0:T(8,128)(2,1)} custom-call(s32[4]{0:T(128)S(1)} %pad_add_fusion.where, bf16[384,3072]{1,0:T(8,128)(2,1)S(1)} %bitcast.133, bf16[8,21,256,512]{3,2,1,0:T(8,128)(2,1)} %refs_5_.23, bf16[8,21,256,512]{3,2,1,0:T(8,128)(2,1)} %refs_5_.23, bf16[8,21,256,512]{3,2,1,0:T(8,128)(2,1)} %refs_5_.23, ...), custom_call_target="tpu_custom_call" | custom-call | flops 2415919104 | bytes 8650752 | tf_op jit(solution)/shard_map/half_send_3/pallas_call | solution.py:168
  48.6 16.3 %collective-permute-done.6.refs_6_ = bf16[4,384,512]{2,1,0:T(8,128)(2,1)} collective-permute-done((bf16[4,384,512]{2,1,0:T(8,128)(2,1)}, bf16[4,384,512]{2,1,0:T(8,128)(2,1)}, u32[]{:S(2)}, u32[]{:S(2)}) %collective-permute-start.6) | collective-permute-done | bytes 1572896 | tf_op jit(solution)/shard_map/ppermute | solution.py:253
  64.9 2.1 collective-permute-start.18
  69.4 6.9 %half_own_1.1.refs_1_ = bf16[512,1536]{1,0:T(8,128)(2,1)S(1)} custom-call(s32[4]{0:T(128)S(1)} %pad_add_fusion.where, bf16[384,3072]{1,0:T(8,128)(2,1)S(1)} %bitcast.134, bf16[8,21,256,512]{3,2,1,0:T(8,128)(2,1)} %refs_5_.23, bf16[8,21,256,512]{3,2,1,0:T(8,128)(2,1)} %refs_5_.23, bf16[8,21,256,512]{3,2,1,0:T(8,128)(2,1)} %refs_5_.23, ...), custom_call_target="tpu_custom_call" | custom-call | flops 2415919104 | bytes 8650752 | tf_op jit(solution)/shard_map/half_own_1/pallas_call | solution.py:168
  76.3 3.5 tiles_1.1
  79.7 7.0 %half_send_4.1 = bf16[4,384,512]{2,1,0:T(8,128)(2,1)} custom-call(s32[4]{0:T(128)S(1)} %pad_add_fusion.where, bf16[384,3072]{1,0:T(8,128)(2,1)S(1)} %bitcast.135, bf16[8,21,256,512]{3,2,1,0:T(8,128)(2,1)} %refs_5_.23, bf16[8,21,256,512]{3,2,1,0:T(8,128)(2,1)} %refs_5_.23, bf16[8,21,256,512]{3,2,1,0:T(8,128)(2,1)} %refs_5_.23, ...), custom_call_target="tpu_custom_call" | custom-call | flops 2415919104 | bytes 8650752 | tf_op jit(solution)/shard_map/half_send_4/pallas_call | solution.py:168
  86.7 11.9 %collective-permute-done.12.refs_6_ = bf16[4,384,512]{2,1,0:T(8,128)(2,1)} collective-permute-done((bf16[4,384,512]{2,1,0:T(8,128)(2,1)}, bf16[4,384,512]{2,1,0:T(8,128)(2,1)}, u32[]{:S(2)}, u32[]{:S(2)}) %collective-permute-start.12) | collective-permute-done | bytes 1572896 | tf_op jit(solution)/shard_map/ppermute | solution.py:253
  98.6 2.1 collective-permute-start.24
  100.7 7.0 %half_send_5.1 = bf16[4,384,512]{2,1,0:T(8,128)(2,1)} custom-call(s32[4]{0:T(128)S(1)} %pad_add_fusion.where, bf16[384,3072]{1,0:T(8,128)(2,1)S(1)} %bitcast.136, bf16[8,21,256,512]{3,2,1,0:T(8,128)(2,1)} %refs_5_.23, bf16[8,21,256,512]{3,2,1,0:T(8,128)(2,1)} %refs_5_.23, bf16[8,21,256,512]{3,2,1,0:T(8,128)(2,1)} %refs_5_.23, ...), custom_call_target="tpu_custom_call" | custom-call | flops 2415919104 | bytes 8650752 | tf_op jit(solution)/shard_map/half_send_5/pallas_call | solution.py:168
  110.9 7.1 %half_own_2.1.refs_2_ = bf16[512,1536]{1,0:T(8,128)(2,1)S(1)} custom-call(s32[4]{0:T(128)S(1)} %pad_add_fusion.where, bf16[384,3072]{1,0:T(8,128)(2,1)S(1)} %bitcast.137, bf16[8,21,256,512]{3,2,1,0:T(8,128)(2,1)} %refs_5_.23, bf16[8,21,256,512]{3,2,1,0:T(8,128)(2,1)} %refs_5_.23, bf16[8,21,256,512]{3,2,1,0:T(8,128)(2,1)} %refs_5_.23, ...), custom_call_target="tpu_custom_call" | custom-call | flops 2415919104 | bytes 8650752 | tf_op jit(solution)/shard_map/half_own_2/pallas_call | solution.py:168
  118.0 14.3 %collective-permute-done.18.refs_6_ = bf16[4,384,512]{2,1,0:T(8,128)(2,1)} collective-permute-done((bf16[4,384,512]{2,1,0:T(8,128)(2,1)}, bf16[4,384,512]{2,1,0:T(8,128)(2,1)}, u32[]{:S(2)}, u32[]{:S(2)}) %collective-permute-start.18) | collective-permute-done | bytes 1572896 | tf_op jit(solution)/shard_map/ppermute | solution.py:253
  132.3 2.1 collective-permute-start.30
  134.4 4.5 %tiles_2.1 = (f32[8,2,3,32,256]{4,3,2,1,0:T(8,128)S(1)}, f32[8,2,3,32,256]{4,3,2,1,0:T(8,128)}) custom-call(s32[4]{0:T(128)S(1)} %pad_add_fusion.where, bf16[512,1536]{1,0:T(8,128)(2,1)S(1)} %half_own_0.1.refs_0_, bf16[512,1536]{1,0:T(8,128)(2,1)S(1)} %copy-done.1, bf16[512,1536]{1,0:T(8,128)(2,1)S(1)} %half_own_2.1.refs_2_), custom_call_target="tpu_custom_call" | custom-call | flops 2415919104 | bytes 7864320 | tf_op jit(solution)/shard_map/tiles_2/pallas_call | solution.py:221
  138.9 2.9 slice_add_fusion.15
  143.3 6.8 %half_own_3.1.refs_3_ = bf16[512,1536]{1,0:T(8,128)(2,1)S(1)} custom-call(s32[4]{0:T(128)S(1)} %pad_add_fusion.where, bf16[384,3072]{1,0:T(8,128)(2,1)S(1)} %bitcast.138, bf16[8,21,256,512]{3,2,1,0:T(8,128)(2,1)} %refs_5_.23, bf16[8,21,256,512]{3,2,1,0:T(8,128)(2,1)} %refs_5_.23, bf16[8,21,256,512]{3,2,1,0:T(8,128)(2,1)} %refs_5_.23, ...), custom_call_target="tpu_custom_call" | custom-call | flops 2415919104 | bytes 8650752 | tf_op jit(solution)/shard_map/half_own_3/pallas_call | solution.py:168
  150.1 5.5 %tiles_3.1 = (f32[8,2,4,32,256]{4,3,2,1,0:T(8,128)S(1)}, f32[8,2,4,32,256]{4,3,2,1,0:T(8,128)}) custom-call(s32[4]{0:T(128)S(1)} %pad_add_fusion.where, bf16[512,1536]{1,0:T(8,128)(2,1)S(1)} %half_own_0.1.refs_0_, bf16[512,1536]{1,0:T(8,128)(2,1)S(1)} %copy-done.1, bf16[512,1536]{1,0:T(8,128)(2,1)S(1)} %half_own_2.1.refs_2_, ...), custom_call_target="tpu_custom_call" | custom-call | flops 3221225472 | bytes 10485760 | tf_op jit(solution)/shard_map/tiles_3/pallas_call | solution.py:221
  155.6 10.4 %collective-permute-done.24.refs_6_ = bf16[4,384,512]{2,1,0:T(8,128)(2,1)} collective-permute-done((bf16[4,384,512]{2,1,0:T(8,128)(2,1)}, bf16[4,384,512]{2,1,0:T(8,128)(2,1)}, u32[]{:S(2)}, u32[]{:S(2)}) %collective-permute-start.24) | collective-permute-done | bytes 1572896 | tf_op jit(solution)/shard_map/ppermute | solution.py:253
  166.0 6.8 %half_own_4.1.refs_4_ = bf16[512,1536]{1,0:T(8,128)(2,1)S(1)} custom-call(s32[4]{0:T(128)S(1)} %pad_add_fusion.where, bf16[384,3072]{1,0:T(8,128)(2,1)S(1)} %bitcast.139, bf16[8,21,256,512]{3,2,1,0:T(8,128)(2,1)} %refs_5_.23, bf16[8,21,256,512]{3,2,1,0:T(8,128)(2,1)} %refs_5_.23, bf16[8,21,256,512]{3,2,1,0:T(8,128)(2,1)} %refs_5_.23, ...), custom_call_target="tpu_custom_call" | custom-call | flops 2415919104 | bytes 8650752 | tf_op jit(solution)/shard_map/half_own_4/pallas_call | solution.py:168
  172.9 6.6 %tiles_4.1 = (f32[8,2,5,32,256]{4,3,2,1,0:T(8,128)S(1)}, f32[8,2,5,32,256]{4,3,2,1,0:T(8,128)}) custom-call(s32[4]{0:T(128)S(1)} %pad_add_fusion.where, bf16[512,1536]{1,0:T(8,128)(2,1)S(1)} %half_own_0.1.refs_0_, bf16[512,1536]{1,0:T(8,128)(2,1)S(1)} %copy-done.1, bf16[512,1536]{1,0:T(8,128)(2,1)S(1)} %half_own_2.1.refs_2_, ...), custom_call_target="tpu_custom_call" | custom-call | flops 4026531840 | bytes 13107200 | tf_op jit(solution)/shard_map/tiles_4/pallas_call | solution.py:221
  179.5 19.4 %collective-permute-done.30.refs_6_ = bf16[4,384,512]{2,1,0:T(8,128)(2,1)} collective-permute-done((bf16[4,384,512]{2,1,0:T(8,128)(2,1)}, bf16[4,384,512]{2,1,0:T(8,128)(2,1)}, u32[]{:S(2)}, u32[]{:S(2)}) %collective-permute-start.30) | collective-permute-done | bytes 1572896 | tf_op jit(solution)/shard_map/ppermute | solution.py:253
  198.9 7.0 %half_own_5.1.refs_5_ = bf16[512,1536]{1,0:T(8,128)(2,1)S(1)} custom-call(s32[4]{0:T(128)S(1)} %pad_add_fusion.where, bf16[384,3072]{1,0:T(8,128)(2,1)S(1)} %bitcast.140, bf16[8,21,256,512]{3,2,1,0:T(8,128)(2,1)} %refs_5_.23, bf16[8,21,256,512]{3,2,1,0:T(8,128)(2,1)} %refs_5_.23, bf16[8,21,256,512]{3,2,1,0:T(8,128)(2,1)} %refs_5_.23, ...), custom_call_target="tpu_custom_call" | custom-call | flops 2415919104 | bytes 8650752 | tf_op jit(solution)/shard_map/half_own_5/pallas_call | solution.py:168
  207.4 7.5 %tiles_5.1 = (f32[8,2,6,32,256]{4,3,2,1,0:T(8,128)S(1)}, f32[8,2,6,32,256]{4,3,2,1,0:T(8,128)}) custom-call(s32[4]{0:T(128)S(1)} %pad_add_fusion.where, bf16[512,1536]{1,0:T(8,128)(2,1)S(1)} %half_own_0.1.refs_0_, bf16[512,1536]{1,0:T(8,128)(2,1)S(1)} %copy-done.1, bf16[512,1536]{1,0:T(8,128)(2,1)S(1)} %half_own_2.1.refs_2_, ...), custom_call_target="tpu_custom_call" | custom-call | flops 4831838208 | bytes 15728640 | tf_op jit(solution)/shard_map/tiles_5/pallas_call | solution.py:221
  219.3 5.7 %collective-permute-done.9 = f32[2,2,2,32,256]{4,3,2,1,0:T(8,128)S(1)} collective-permute-done((f32[2,2,2,32,256]{4,3,2,1,0:T(8,128)S(1)}, f32[2,2,2,32,256]{4,3,2,1,0:T(8,128)S(1)}, u32[]{:S(2)}, u32[]{:S(2)}) %collective-permute-start.9) | collective-permute-done | bytes 262176 | tf_op jit(solution)/shard_map/ppermute | solution.py:260
  225.0 2.7 collective-permute-start.4
  233.8 2.9 collective-permute-done.10
  238.3 2.3 collective-permute-done.5
  242.2 2.7 collective-permute-done.11
  244.9 5.3 %collective-permute-done.14 = f32[4,2,3,32,256]{4,3,2,1,0:T(8,128)S(1)} collective-permute-done((f32[4,2,3,32,256]{4,3,2,1,0:T(8,128)S(1)}, f32[4,2,3,32,256]{4,3,2,1,0:T(8,128)S(1)}, u32[]{:S(2)}, u32[]{:S(2)}) %collective-permute-start.14) | collective-permute-done | bytes 786464 | tf_op jit(solution)/shard_map/ppermute | solution.py:260
  252.2 18.4 %collective-permute-done.20 = f32[4,2,4,32,256]{4,3,2,1,0:T(8,128)S(1)} collective-permute-done((f32[4,2,4,32,256]{4,3,2,1,0:T(8,128)S(1)}, f32[4,2,4,32,256]{4,3,2,1,0:T(8,128)S(1)}, u32[]{:S(2)}, u32[]{:S(2)}) %collective-permute-start.20) | collective-permute-done | bytes 1048608 | tf_op jit(solution)/shard_map/ppermute | solution.py:260
  272.4 2.2 slice_add_fusion.3
  277.6 2.6 collective-permute-start.16
  280.2 5.8 %collective-permute-done.16 = f32[1,2,3,32,256]{4,3,2,1,0:T(8,128)S(1)} collective-permute-done((f32[1,2,3,32,256]{4,3,2,1,0:T(8,128)S(1)}, f32[1,2,3,32,256]{4,3,2,1,0:T(8,128)S(1)}, u32[]{:S(2)}, u32[]{:S(2)}) %collective-permute-start.16) | collective-permute-done | bytes 196640 | tf_op jit(solution)/shard_map/ppermute | solution.py:260
  287.7 3.3 collective-permute-start.22
  291.0 15.4 %collective-permute-done.26 = f32[4,2,5,32,256]{4,3,2,1,0:T(8,128)S(1)} collective-permute-done((f32[4,2,5,32,256]{4,3,2,1,0:T(8,128)S(1)}, f32[4,2,5,32,256]{4,3,2,1,0:T(8,128)S(1)}, u32[]{:S(2)}, u32[]{:S(2)}) %collective-permute-start.26) | collective-permute-done | bytes 1310752 | tf_op jit(solution)/shard_map/ppermute | solution.py:260
  308.9 27.8 %collective-permute-done.32 = f32[4,2,6,32,256]{4,3,2,1,0:T(8,128)S(1)} collective-permute-done((f32[4,2,6,32,256]{4,3,2,1,0:T(8,128)S(1)}, f32[4,2,6,32,256]{4,3,2,1,0:T(8,128)S(1)}, u32[]{:S(2)}, u32[]{:S(2)}) %collective-permute-start.32) | collective-permute-done | bytes 1572896 | tf_op jit(solution)/shard_map/ppermute | solution.py:260
  337.6 2.6 collective-permute-start.28
  340.3 18.0 %collective-permute-done.28 = f32[1,2,5,32,256]{4,3,2,1,0:T(8,128)S(1)} collective-permute-done((f32[1,2,5,32,256]{4,3,2,1,0:T(8,128)S(1)}, f32[1,2,5,32,256]{4,3,2,1,0:T(8,128)S(1)}, u32[]{:S(2)}, u32[]{:S(2)}) %collective-permute-start.28) | collective-permute-done | bytes 327712 | tf_op jit(solution)/shard_map/ppermute | solution.py:260
  360.2 3.1 collective-permute-start.34
  363.7 15.4 %collective-permute-done.34 = f32[1,2,6,32,256]{4,3,2,1,0:T(8,128)S(1)} collective-permute-done((f32[1,2,6,32,256]{4,3,2,1,0:T(8,128)S(1)}, f32[1,2,6,32,256]{4,3,2,1,0:T(8,128)S(1)}, u32[]{:S(2)}, u32[]{:S(2)}) %collective-permute-start.34) | collective-permute-done | bytes 393248 | tf_op jit(solution)/shard_map/ppermute | solution.py:260
  380.6 5.1 %collective-permute-done.35 = f32[1,6,32,256]{3,2,1,0:T(8,128)S(1)} collective-permute-done((f32[1,6,32,256]{3,2,1,0:T(8,128)S(1)}, f32[1,6,32,256]{3,2,1,0:T(8,128)S(1)}, u32[]{:S(2)}, u32[]{:S(2)}) %collective-permute-start.35) | collective-permute-done | bytes 196640 | tf_op jit(solution)/shard_map/ppermute | solution.py:268
  (120 shorter events, 41.2 us)
Async XLA Ops:
  9.6 21.6 %collective-permute-start = (bf16[4,384,256]{2,1,0:T(8,128)(2,1)}, bf16[4,384,256]{2,1,0:T(8,128)(2,1)}, u32[]{:S(2)}, u32[]{:S(2)}) collective-permute-start(bf16[4,384,256]{2,1,0:T(8,128)(2,1)} %half_send_0.1), channel_id=1, source_target_pairs={{0,1},{1,0},{2,3},{3,2},{4,5},{5,4},{6,7},{7,6},{8,9},{9,8},{10,11... | collective-permute-start | bytes 2359304 | tf_op jit(solution)/shard_map/ppermute | solution.py:253
  19.5 45.4 %collective-permute-start.6 = (bf16[4,384,512]{2,1,0:T(8,128)(2,1)}, bf16[4,384,512]{2,1,0:T(8,128)(2,1)}, u32[]{:S(2)}, u32[]{:S(2)}) collective-permute-start(bf16[4,384,512]{2,1,0:T(8,128)(2,1)} %half_send_1.1), channel_id=1, source_target_pairs={{0,1},{1,0},{2,3},{3,2},{4,5},{5,4},{6,7},{7,6},{8,9},{9,8},{10,11... | collective-permute-start | bytes 4718600 | tf_op jit(solution)/shard_map/ppermute | solution.py:253
  31.2 67.4 %collective-permute-start.12 = (bf16[4,384,512]{2,1,0:T(8,128)(2,1)}, bf16[4,384,512]{2,1,0:T(8,128)(2,1)}, u32[]{:S(2)}, u32[]{:S(2)}) collective-permute-start(bf16[4,384,512]{2,1,0:T(8,128)(2,1)} %half_send_2.1), channel_id=1, source_target_pairs={{0,1},{1,0},{2,3},{3,2},{4,5},{5,4},{6,7},{7,6},{8,9},{9,8},{10,11... | collective-permute-start | bytes 4718600 | tf_op jit(solution)/shard_map/ppermute | solution.py:253
  41.6 25.4 %collective-permute-start.1 = (f32[8,2,1,32,256]{4,3,2,1,0:T(8,128)S(1)}, f32[8,2,1,32,256]{4,3,2,1,0:T(8,128)S(1)}, u32[]{:S(2)}, u32[]{:S(2)}) collective-permute-start(f32[8,2,1,32,256]{4,3,2,1,0:T(8,128)S(1)} %get-tuple-element.27), channel_id=1, source_target_pairs={{0,2},{2,0},{4,6},{6,4},{8,10},{10,8},{12,14},{14,12},{16,18},{18,... | collective-permute-start | bytes 1572872 | tf_op jit(solution)/shard_map/ppermute | solution.py:260
  64.9 67.4 %collective-permute-start.18 = (bf16[4,384,512]{2,1,0:T(8,128)(2,1)}, bf16[4,384,512]{2,1,0:T(8,128)(2,1)}, u32[]{:S(2)}, u32[]{:S(2)}) collective-permute-start(bf16[4,384,512]{2,1,0:T(8,128)(2,1)} %half_send_3.1), channel_id=1, source_target_pairs={{0,1},{1,0},{2,3},{3,2},{4,5},{5,4},{6,7},{7,6},{8,9},{9,8},{10,11... | collective-permute-start | bytes 4718600 | tf_op jit(solution)/shard_map/ppermute | solution.py:253
  67.8 39.8 %collective-permute-start.2 = (f32[4,2,1,32,256]{4,3,2,1,0:T(8,128)}, f32[4,2,1,32,256]{4,3,2,1,0:T(8,128)}, u32[]{:S(2)}, u32[]{:S(2)}) collective-permute-start(f32[4,2,1,32,256]{4,3,2,1,0:T(8,128)} %get-tuple-element.72), channel_id=1, source_target_pairs={{0,4},{2,6},{4,0},{6,2},{8,12},{10,14},{12,8},{14,10},{16,20},{18,... | collective-permute-start | bytes 786440 | tf_op jit(solution)/shard_map/ppermute | solution.py:260
  76.3 3.5 copy-start
  79.7 59.2 %collective-permute-start.7 = (f32[8,2,2,32,256]{4,3,2,1,0:T(8,128)}, f32[8,2,2,32,256]{4,3,2,1,0:T(8,128)}, u32[]{:S(2)}, u32[]{:S(2)}) collective-permute-start(f32[8,2,2,32,256]{4,3,2,1,0:T(8,128)} %get-tuple-element.30), channel_id=1, source_target_pairs={{0,2},{2,0},{4,6},{6,4},{8,10},{10,8},{12,14},{14,12},{16,18},{18,... | collective-permute-start | bytes 3145736 | tf_op jit(solution)/shard_map/ppermute | solution.py:260
  86.7 20.9 %copy-start.10 = (f32[4,2,1,32,256]{4,3,2,1,0:T(8,128)S(1)}, f32[4,2,1,32,256]{4,3,2,1,0:T(8,128)}, u32[]{:S(2)}) copy-start(f32[4,2,1,32,256]{4,3,2,1,0:T(8,128)} %get-tuple-element.71) | copy-start | bytes 786436
  98.6 67.4 %collective-permute-start.24 = (bf16[4,384,512]{2,1,0:T(8,128)(2,1)}, bf16[4,384,512]{2,1,0:T(8,128)(2,1)}, u32[]{:S(2)}, u32[]{:S(2)}) collective-permute-start(bf16[4,384,512]{2,1,0:T(8,128)(2,1)} %half_send_4.1), channel_id=1, source_target_pairs={{0,1},{1,0},{2,3},{3,2},{4,5},{5,4},{6,7},{7,6},{8,9},{9,8},{10,11... | collective-permute-start | bytes 4718600 | tf_op jit(solution)/shard_map/ppermute | solution.py:253
  109.4 25.0 %copy-start.1 = (bf16[512,1536]{1,0:T(8,128)(2,1)S(1)}, bf16[512,1536]{1,0:T(8,128)(2,1)}, u32[]{:S(2)}) copy-start(bf16[512,1536]{1,0:T(8,128)(2,1)} %copy-done) | copy-start | bytes 4718596
  109.4 107.2 %collective-permute-start.3 = (f32[2,2,1,32,256]{4,3,2,1,0:T(8,128)}, f32[2,2,1,32,256]{4,3,2,1,0:T(8,128)}, u32[]{:S(2)}, u32[]{:S(2)}) collective-permute-start(f32[2,2,1,32,256]{4,3,2,1,0:T(8,128)} %get-tuple-element.78), channel_id=1, source_target_pairs={{0,8},{2,10},{4,12},{6,14},{8,0},{10,2},{12,4},{14,6},{16,24},{18,... | collective-permute-start | bytes 393224 | tf_op jit(solution)/shard_map/ppermute | solution.py:260
  132.3 66.6 %collective-permute-start.30 = (bf16[4,384,512]{2,1,0:T(8,128)(2,1)}, bf16[4,384,512]{2,1,0:T(8,128)(2,1)}, u32[]{:S(2)}, u32[]{:S(2)}) collective-permute-start(bf16[4,384,512]{2,1,0:T(8,128)(2,1)} %half_send_5.1), channel_id=1, source_target_pairs={{0,1},{1,0},{2,3},{3,2},{4,5},{5,4},{6,7},{7,6},{8,9},{9,8},{10,11... | collective-permute-start | bytes 4718600 | tf_op jit(solution)/shard_map/ppermute | solution.py:253
  138.9 2.9 copy-start.7
  138.9 88.9 %collective-permute-start.13 = (f32[8,2,3,32,256]{4,3,2,1,0:T(8,128)}, f32[8,2,3,32,256]{4,3,2,1,0:T(8,128)}, u32[]{:S(2)}, u32[]{:S(2)}) collective-permute-start(f32[8,2,3,32,256]{4,3,2,1,0:T(8,128)} %get-tuple-element.34), channel_id=1, source_target_pairs={{0,2},{2,0},{4,6},{6,4},{8,10},{10,8},{12,14},{14,12},{16,18},{18,... | collective-permute-start | bytes 4718600 | tf_op jit(solution)/shard_map/ppermute | solution.py:260
  141.8 73.1 %collective-permute-start.8 = (f32[4,2,2,32,256]{4,3,2,1,0:T(8,128)}, f32[4,2,2,32,256]{4,3,2,1,0:T(8,128)}, u32[]{:S(2)}, u32[]{:S(2)}) collective-permute-start(f32[4,2,2,32,256]{4,3,2,1,0:T(8,128)} %get-tuple-element.60), channel_id=1, source_target_pairs={{0,4},{2,6},{4,0},{6,2},{8,12},{10,14},{12,8},{14,10},{16,20},{18,... | collective-permute-start | bytes 1572872 | tf_op jit(solution)/shard_map/ppermute | solution.py:260
  150.1 5.5 %copy-start.2 = (bf16[512,1536]{1,0:T(8,128)(2,1)}, bf16[512,1536]{1,0:T(8,128)(2,1)S(1)}, u32[]{:S(2)}) copy-start(bf16[512,1536]{1,0:T(8,128)(2,1)S(1)} %half_own_3.1.refs_3_) | copy-start | bytes 4718596
  166.0 6.8 %copy-start.3 = (bf16[512,1536]{1,0:T(8,128)(2,1)S(1)}, bf16[512,1536]{1,0:T(8,128)(2,1)}, u32[]{:S(2)}) copy-start(bf16[512,1536]{1,0:T(8,128)(2,1)} %copy-done.2) | copy-start | bytes 4718596
  166.0 63.7 %collective-permute-start.19 = (f32[8,2,4,32,256]{4,3,2,1,0:T(8,128)}, f32[8,2,4,32,256]{4,3,2,1,0:T(8,128)}, u32[]{:S(2)}, u32[]{:S(2)}) collective-permute-start(f32[8,2,4,32,256]{4,3,2,1,0:T(8,128)} %get-tuple-element.38), channel_id=1, source_target_pairs={{0,2},{2,0},{4,6},{6,4},{8,10},{10,8},{12,14},{14,12},{16,18},{18,... | collective-permute-start | bytes 6291464 | tf_op jit(solution)/shard_map/ppermute | solution.py:260
  172.9 6.6 %copy-start.5 = (bf16[512,1536]{1,0:T(8,128)(2,1)}, bf16[512,1536]{1,0:T(8,128)(2,1)S(1)}, u32[]{:S(2)}) copy-start(bf16[512,1536]{1,0:T(8,128)(2,1)S(1)} %half_own_4.1.refs_4_) | copy-start | bytes 4718596
  198.9 7.1 %copy-start.6 = (bf16[512,1536]{1,0:T(8,128)(2,1)S(1)}, bf16[512,1536]{1,0:T(8,128)(2,1)}, u32[]{:S(2)}) copy-start(bf16[512,1536]{1,0:T(8,128)(2,1)} %copy-done.5) | copy-start | bytes 4718596
  198.9 73.5 %collective-permute-start.25 = (f32[8,2,5,32,256]{4,3,2,1,0:T(8,128)}, f32[8,2,5,32,256]{4,3,2,1,0:T(8,128)}, u32[]{:S(2)}, u32[]{:S(2)}) collective-permute-start(f32[8,2,5,32,256]{4,3,2,1,0:T(8,128)} %get-tuple-element.41), channel_id=1, source_target_pairs={{0,2},{2,0},{4,6},{6,4},{8,10},{10,8},{12,14},{14,12},{16,18},{18,... | collective-permute-start | bytes 7864328 | tf_op jit(solution)/shard_map/ppermute | solution.py:260
  206.0 1.4 copy-start.4
  207.4 8.0 %copy-start.9 = (f32[4,2,2,32,256]{4,3,2,1,0:T(8,128)S(1)}, f32[4,2,2,32,256]{4,3,2,1,0:T(8,128)}, u32[]{:S(2)}) copy-start(f32[4,2,2,32,256]{4,3,2,1,0:T(8,128)} %get-tuple-element.59) | copy-start | bytes 1572868
  207.4 11.1 %copy-start.11 = (f32[2,2,1,32,256]{4,3,2,1,0:T(8,128)S(1)}, f32[2,2,1,32,256]{4,3,2,1,0:T(8,128)}, u32[]{:S(2)}) copy-start(f32[2,2,1,32,256]{4,3,2,1,0:T(8,128)} %get-tuple-element.77) | copy-start | bytes 393220
  214.9 13.2 %copy-start.8 = (f32[8,2,3,32,256]{4,3,2,1,0:T(8,128)S(1)}, f32[8,2,3,32,256]{4,3,2,1,0:T(8,128)}, u32[]{:S(2)}) copy-start(f32[8,2,3,32,256]{4,3,2,1,0:T(8,128)} %copy-done.7) | copy-start | bytes 4718596
  214.9 61.3 %collective-permute-start.31 = (f32[8,2,6,32,256]{4,3,2,1,0:T(8,128)}, f32[8,2,6,32,256]{4,3,2,1,0:T(8,128)S(1)}, u32[]{:S(2)}, u32[]{:S(2)}) collective-permute-start(f32[8,2,6,32,256]{4,3,2,1,0:T(8,128)} %get-tuple-element.44), channel_id=1, source_target_pairs={{0,2},{2,0},{4,6},{6,4},{8,10},{10,8},{12,14},{14,12},{16,18},{18,... | collective-permute-start | bytes 9437192 | tf_op jit(solution)/shard_map/ppermute | solution.py:260
  216.5 8.5 %collective-permute-start.9 = (f32[2,2,2,32,256]{4,3,2,1,0:T(8,128)S(1)}, f32[2,2,2,32,256]{4,3,2,1,0:T(8,128)S(1)}, u32[]{:S(2)}, u32[]{:S(2)}) collective-permute-start(f32[2,2,2,32,256]{4,3,2,1,0:T(8,128)S(1)} %get-tuple-element.70), channel_id=1, source_target_pairs={{0,8},{2,10},{4,12},{6,14},{8,0},{10,2},{12,4},{14,6},{16,24},{18,... | collective-permute-start | bytes 786440 | tf_op jit(solution)/shard_map/ppermute | solution.py:260
  225.0 8.4 %collective-permute-start.4 = (f32[1,2,1,32,256]{4,3,2,1,0:T(8,128)S(1)}, f32[1,2,1,32,256]{4,3,2,1,0:T(8,128)S(1)}, u32[]{:S(2)}, u32[]{:S(2)}) collective-permute-start(f32[1,2,1,32,256]{4,3,2,1,0:T(8,128)S(1)} %get-tuple-element.80), channel_id=1, source_target_pairs={{0,16},{2,18},{4,20},{6,22},{8,24},{10,26},{12,28},{14,30},{16,0},... | collective-permute-start | bytes 196616 | tf_op jit(solution)/shard_map/ppermute | solution.py:260
  227.8 8.9 %collective-permute-start.10 = (f32[1,2,2,32,256]{4,3,2,1,0:T(8,128)S(1)}, f32[1,2,2,32,256]{4,3,2,1,0:T(8,128)S(1)}, u32[]{:S(2)}, u32[]{:S(2)}) collective-permute-start(f32[1,2,2,32,256]{4,3,2,1,0:T(8,128)S(1)} %get-tuple-element.76), channel_id=1, source_target_pairs={{0,16},{2,18},{4,20},{6,22},{8,24},{10,26},{12,28},{14,30},{16,0},... | collective-permute-start | bytes 393224 | tf_op jit(solution)/shard_map/ppermute | solution.py:260
  229.7 20.5 %collective-permute-start.14 = (f32[4,2,3,32,256]{4,3,2,1,0:T(8,128)S(1)}, f32[4,2,3,32,256]{4,3,2,1,0:T(8,128)S(1)}, u32[]{:S(2)}, u32[]{:S(2)}) collective-permute-start(f32[4,2,3,32,256]{4,3,2,1,0:T(8,128)S(1)} %get-tuple-element.54), channel_id=1, source_target_pairs={{0,4},{2,6},{4,0},{6,2},{8,12},{10,14},{12,8},{14,10},{16,20},{18,... | collective-permute-start | bytes 2359304 | tf_op jit(solution)/shard_map/ppermute | solution.py:260
  233.4 37.1 %collective-permute-start.20 = (f32[4,2,4,32,256]{4,3,2,1,0:T(8,128)S(1)}, f32[4,2,4,32,256]{4,3,2,1,0:T(8,128)S(1)}, u32[]{:S(2)}, u32[]{:S(2)}) collective-permute-start(f32[4,2,4,32,256]{4,3,2,1,0:T(8,128)S(1)} %get-tuple-element.50), channel_id=1, source_target_pairs={{0,4},{2,6},{4,0},{6,2},{8,12},{10,14},{12,8},{14,10},{16,20},{18,... | collective-permute-start | bytes 3145736 | tf_op jit(solution)/shard_map/ppermute | solution.py:260
  236.7 3.9 %collective-permute-start.5 = (f32[1,1,32,256]{3,2,1,0:T(8,128)S(1)}, f32[1,1,32,256]{3,2,1,0:T(8,128)S(1)}, u32[]{:S(2)}, u32[]{:S(2)}) collective-permute-start(f32[1,1,32,256]{3,2,1,0:T(8,128)S(1)} %fusion.15), channel_id=1, source_target_pairs={{0,1},{1,0},{2,3},{3,2},{4,5},{5,4},{6,7},{7,6},{8,9},{9,8},{10,11... | collective-permute-start | bytes 98312 | tf_op jit(solution)/shard_map/ppermute | solution.py:268
  240.6 4.3 %collective-permute-start.11 = (f32[1,2,32,256]{3,2,1,0:T(8,128)S(1)}, f32[1,2,32,256]{3,2,1,0:T(8,128)S(1)}, u32[]{:S(2)}, u32[]{:S(2)}) collective-permute-start(f32[1,2,32,256]{3,2,1,0:T(8,128)S(1)} %fusion.12), channel_id=1, source_target_pairs={{0,1},{1,0},{2,3},{3,2},{4,5},{5,4},{6,7},{7,6},{8,9},{9,8},{10,11... | collective-permute-start | bytes 196616 | tf_op jit(solution)/shard_map/ppermute | solution.py:268
  250.4 27.1 %collective-permute-start.15 = (f32[2,2,3,32,256]{4,3,2,1,0:T(8,128)S(1)}, f32[2,2,3,32,256]{4,3,2,1,0:T(8,128)S(1)}, u32[]{:S(2)}, u32[]{:S(2)}) collective-permute-start(f32[2,2,3,32,256]{4,3,2,1,0:T(8,128)S(1)} %get-tuple-element.64), channel_id=1, source_target_pairs={{0,8},{2,10},{4,12},{6,14},{8,0},{10,2},{12,4},{14,6},{16,24},{18,... | collective-permute-start | bytes 1179656 | tf_op jit(solution)/shard_map/ppermute | solution.py:260
  270.7 16.9 %collective-permute-start.21 = (f32[2,2,4,32,256]{4,3,2,1,0:T(8,128)S(1)}, f32[2,2,4,32,256]{4,3,2,1,0:T(8,128)S(1)}, u32[]{:S(2)}, u32[]{:S(2)}) collective-permute-start(f32[2,2,4,32,256]{4,3,2,1,0:T(8,128)S(1)} %get-tuple-element.58), channel_id=1, source_target_pairs={{0,8},{2,10},{4,12},{6,14},{8,0},{10,2},{12,4},{14,6},{16,24},{18,... | collective-permute-start | bytes 1572872 | tf_op jit(solution)/shard_map/ppermute | solution.py:260
  274.7 31.8 %collective-permute-start.26 = (f32[4,2,5,32,256]{4,3,2,1,0:T(8,128)S(1)}, f32[4,2,5,32,256]{4,3,2,1,0:T(8,128)S(1)}, u32[]{:S(2)}, u32[]{:S(2)}) collective-permute-start(f32[4,2,5,32,256]{4,3,2,1,0:T(8,128)S(1)} %get-tuple-element.48), channel_id=1, source_target_pairs={{0,4},{2,6},{4,0},{6,2},{8,12},{10,14},{12,8},{14,10},{16,20},{18,... | collective-permute-start | bytes 3932168 | tf_op jit(solution)/shard_map/ppermute | solution.py:260
  276.9 59.7 %collective-permute-start.32 = (f32[4,2,6,32,256]{4,3,2,1,0:T(8,128)S(1)}, f32[4,2,6,32,256]{4,3,2,1,0:T(8,128)S(1)}, u32[]{:S(2)}, u32[]{:S(2)}) collective-permute-start(f32[4,2,6,32,256]{4,3,2,1,0:T(8,128)S(1)} %get-tuple-element.46), channel_id=1, source_target_pairs={{0,4},{2,6},{4,0},{6,2},{8,12},{10,14},{12,8},{14,10},{16,20},{18,... | collective-permute-start | bytes 4718600 | tf_op jit(solution)/shard_map/ppermute | solution.py:260
  277.6 8.4 %collective-permute-start.16 = (f32[1,2,3,32,256]{4,3,2,1,0:T(8,128)S(1)}, f32[1,2,3,32,256]{4,3,2,1,0:T(8,128)S(1)}, u32[]{:S(2)}, u32[]{:S(2)}) collective-permute-start(f32[1,2,3,32,256]{4,3,2,1,0:T(8,128)S(1)} %get-tuple-element.74), channel_id=1, source_target_pairs={{0,16},{2,18},{4,20},{6,22},{8,24},{10,26},{12,28},{14,30},{16,0},... | collective-permute-start | bytes 589832 | tf_op jit(solution)/shard_map/ppermute | solution.py:260
  286.0 21.1 %collective-permute-start.17 = (f32[1,3,32,256]{3,2,1,0:T(8,128)S(1)}, f32[1,3,32,256]{3,2,1,0:T(8,128)S(1)}, u32[]{:S(2)}, u32[]{:S(2)}) collective-permute-start(f32[1,3,32,256]{3,2,1,0:T(8,128)S(1)} %fusion.9), channel_id=1, source_target_pairs={{0,1},{1,0},{2,3},{3,2},{4,5},{5,4},{6,7},{7,6},{8,9},{9,8},{10,11... | collective-permute-start | bytes 294920 | tf_op jit(solution)/shard_map/ppermute | solution.py:268
  287.7 19.5 %collective-permute-start.22 = (f32[1,2,4,32,256]{4,3,2,1,0:T(8,128)S(1)}, f32[1,2,4,32,256]{4,3,2,1,0:T(8,128)S(1)}, u32[]{:S(2)}, u32[]{:S(2)}) collective-permute-start(f32[1,2,4,32,256]{4,3,2,1,0:T(8,128)S(1)} %get-tuple-element.68), channel_id=1, source_target_pairs={{0,16},{2,18},{4,20},{6,22},{8,24},{10,26},{12,28},{14,30},{16,0},... | collective-permute-start | bytes 786440 | tf_op jit(solution)/shard_map/ppermute | solution.py:260
  306.7 30.9 %collective-permute-start.27 = (f32[2,2,5,32,256]{4,3,2,1,0:T(8,128)S(1)}, f32[2,2,5,32,256]{4,3,2,1,0:T(8,128)S(1)}, u32[]{:S(2)}, u32[]{:S(2)}) collective-permute-start(f32[2,2,5,32,256]{4,3,2,1,0:T(8,128)S(1)} %get-tuple-element.56), channel_id=1, source_target_pairs={{0,8},{2,10},{4,12},{6,14},{8,0},{10,2},{12,4},{14,6},{16,24},{18,... | collective-permute-start | bytes 1966088 | tf_op jit(solution)/shard_map/ppermute | solution.py:260
  307.2 33.0 %collective-permute-start.23 = (f32[1,4,32,256]{3,2,1,0:T(8,128)S(1)}, f32[1,4,32,256]{3,2,1,0:T(8,128)S(1)}, u32[]{:S(2)}, u32[]{:S(2)}) collective-permute-start(f32[1,4,32,256]{3,2,1,0:T(8,128)S(1)} %fusion.6), channel_id=1, source_target_pairs={{0,1},{1,0},{2,3},{3,2},{4,5},{5,4},{6,7},{7,6},{8,9},{9,8},{10,11... | collective-permute-start | bytes 393224 | tf_op jit(solution)/shard_map/ppermute | solution.py:268
  337.0 23.1 %collective-permute-start.33 = (f32[2,2,6,32,256]{4,3,2,1,0:T(8,128)S(1)}, f32[2,2,6,32,256]{4,3,2,1,0:T(8,128)S(1)}, u32[]{:S(2)}, u32[]{:S(2)}) collective-permute-start(f32[2,2,6,32,256]{4,3,2,1,0:T(8,128)S(1)} %get-tuple-element.52), channel_id=1, source_target_pairs={{0,8},{2,10},{4,12},{6,14},{8,0},{10,2},{12,4},{14,6},{16,24},{18,... | collective-permute-start | bytes 2359304 | tf_op jit(solution)/shard_map/ppermute | solution.py:260
  337.6 20.6 %collective-permute-start.28 = (f32[1,2,5,32,256]{4,3,2,1,0:T(8,128)S(1)}, f32[1,2,5,32,256]{4,3,2,1,0:T(8,128)S(1)}, u32[]{:S(2)}, u32[]{:S(2)}) collective-permute-start(f32[1,2,5,32,256]{4,3,2,1,0:T(8,128)S(1)} %get-tuple-element.66), channel_id=1, source_target_pairs={{0,16},{2,18},{4,20},{6,22},{8,24},{10,26},{12,28},{14,30},{16,0},... | collective-permute-start | bytes 983048 | tf_op jit(solution)/shard_map/ppermute | solution.py:260
  358.3 5.4 %collective-permute-start.29 = (f32[1,5,32,256]{3,2,1,0:T(8,128)S(1)}, f32[1,5,32,256]{3,2,1,0:T(8,128)S(1)}, u32[]{:S(2)}, u32[]{:S(2)}) collective-permute-start(f32[1,5,32,256]{3,2,1,0:T(8,128)S(1)} %fusion.3), channel_id=1, source_target_pairs={{0,1},{1,0},{2,3},{3,2},{4,5},{5,4},{6,7},{7,6},{8,9},{9,8},{10,11... | collective-permute-start | bytes 491528 | tf_op jit(solution)/shard_map/ppermute | solution.py:268
  360.2 18.9 %collective-permute-start.34 = (f32[1,2,6,32,256]{4,3,2,1,0:T(8,128)S(1)}, f32[1,2,6,32,256]{4,3,2,1,0:T(8,128)S(1)}, u32[]{:S(2)}, u32[]{:S(2)}) collective-permute-start(f32[1,2,6,32,256]{4,3,2,1,0:T(8,128)S(1)} %get-tuple-element.62), channel_id=1, source_target_pairs={{0,16},{2,18},{4,20},{6,22},{8,24},{10,26},{12,28},{14,30},{16,0},... | collective-permute-start | bytes 1179656 | tf_op jit(solution)/shard_map/ppermute | solution.py:260
  379.2 6.5 %collective-permute-start.35 = (f32[1,6,32,256]{3,2,1,0:T(8,128)S(1)}, f32[1,6,32,256]{3,2,1,0:T(8,128)S(1)}, u32[]{:S(2)}, u32[]{:S(2)}) collective-permute-start(f32[1,6,32,256]{3,2,1,0:T(8,128)S(1)} %fusion), channel_id=1, source_target_pairs={{0,1},{1,0},{2,3},{3,2},{4,5},{5,4},{6,7},{7,6},{8,9},{9,8},{10,11... | collective-permute-start | bytes 589832 | tf_op jit(solution)/shard_map/ppermute | solution.py:268
  (1 other events, 0.8 us)

commit v2 on v1

--- a/solution.py
+++ b/solution.py
@@ -95,6 +95,16 @@
     )
 
 VMEM_LIMIT = 40 * 1024 * 1024
+
+
+def took(microseconds):
+    return pl.CostEstimate(
+        flops=int(microseconds * 1.15e9), bytes_accessed=1, transcendentals=0
+    )
+
+
+DEPTH = 2
+OWN, SEND, TILE_COST = 20, 1, 0.1
 
 
 def tile_at(row_index, col_index):
@@ -176,68 +186,110 @@
             scratch_shapes=[pltpu.VMEM((occ_count, tile_size), jnp.float32)],
         ),
         compiler_params=pltpu.CompilerParams(vmem_limit_bytes=VMEM_LIMIT),
-        cost_estimate=pl.CostEstimate(
-            flops=2 * count * NB * row_width * tile_size * occ_count,
-            bytes_accessed=count * NB * row_width * tile_size * 2 + coeffs.size * 2,
-            transcendentals=0,
-        ),
+        cost_estimate=took(OWN if owned else SEND),
         name=f"half_{'own' if owned else 'send'}_{block}",
     )(where, *args)
 
 
-def bit_reverse(value, bits):
-    return sum(((value >> bit) & 1) << (bits - 1 - bit) for bit in range(bits))
-
-
-def tile_kernel(bits, where, *refs):
-    halves, (keep, send, total) = refs[:-3], refs[-3:]
-    parts = 2**bits
-    rows, cols = keep.shape[3:]
-    for at, left in enumerate(halves):
-        total[...] = lax.dot_general(
-            left[...],
-            halves[-1][...],
-            (((1,), (1,)), ((), ())),
-            preferred_element_type=jnp.float32,
-        )
-        for place in range(parts):
-            out = keep if place < parts // 2 else send
-            owner = lax.bitwise_xor(where[3], jnp.int32(bit_reverse(place, bits)))
-            picked = pl.ds(pl.multiple_of(owner * rows, rows), rows)
-            for side in range(2):
-                half = lax.bitwise_xor(where[0], jnp.int32(side))
-                out[place % (parts // 2), side, at] = total[
-                    picked, pl.ds(pl.multiple_of(half * cols, cols), cols)
-                ]
-
-
-def tile_call(bits, where, halves):
-    parts = 2**bits
+def tile_groups(block, bits):
+    plain = tuple(range(bits))
+    if block < NB - 1 or bits < 3:
+        return [(tuple(range(block + 1)), plain)]
+    turned = (0,) + tuple(range(2, bits)) + (1,)
+    middle = (block + 1) // 2
+    return [(tuple(range(middle)), plain), (tuple(range(middle, block + 1)), turned)]
+
+
+def relative_owner(place, order):
+    bits = len(order)
+    return sum(((place >> (bits - 1 - step)) & 1) << order[step] for step in range(bits))
+
+
+def tile_kernel(groups, where, *refs):
+    count = sum(len(members) for members, _ in groups)
+    halves, outs, total = refs[:count], refs[count:-1], refs[-1]
+    for group, (members, order) in enumerate(groups):
+        keep, send = outs[2 * group : 2 * group + 2]
+        parts = 2 ** len(order)
+        rows, cols = keep.shape[3:]
+        for at, tile in enumerate(members):
+            total[...] = lax.dot_general(
+                halves[tile][...],
+                halves[-1][...],
+                (((1,), (1,)), ((), ())),
+                preferred_element_type=jnp.float32,
+            )
+            for place in range(parts):
+                out = keep if place < parts // 2 else send
+                owner = lax.bitwise_xor(where[3], jnp.int32(relative_owner(place, order)))
+                picked = pl.ds(pl.multiple_of(owner * rows, rows), rows)
+                for side in range(2):
+                    half = lax.bitwise_xor(where[0], jnp.int32(side))
+                    out[place % (parts // 2), side, at] = total[
+                        picked, pl.ds(pl.multiple_of(half * cols, cols), cols)
+                    ]
+
+
+def tile_call(groups, where, halves):
     tile_size, depth = halves[0].shape
     count = len(halves)
-    out = jax.ShapeDtypeStruct(
-        (parts // 2, 2, count, tile_size // parts, tile_size // 2), jnp.float32
-    )
+    parts = 2 ** len(groups[0][1])
+    outs = []
+    for members, _ in groups:
+        outs += [
+            jax.ShapeDtypeStruct(
+                (parts // 2, 2, len(members), tile_size // parts, tile_size // 2), jnp.float32
+            )
+        ] * 2
     return pl.pallas_call(
-        functools.partial(tile_kernel, bits),
-        out_shape=[out, out],
+        functools.partial(tile_kernel, groups),
+        out_shape=outs,
         in_specs=[pl.BlockSpec(memory_space=pltpu.SMEM)]
         + [pl.BlockSpec(memory_space=pltpu.VMEM)] * count,
-        out_specs=[pl.BlockSpec(memory_space=pltpu.VMEM)] * 2,
+        out_specs=[pl.BlockSpec(memory_space=pltpu.VMEM)] * len(outs),
         scratch_shapes=[pltpu.VMEM((tile_size, tile_size), jnp.float32)],
         compiler_params=pltpu.CompilerParams(vmem_limit_bytes=VMEM_LIMIT),
-        cost_estimate=pl.CostEstimate(
-            flops=2 * count * tile_size * tile_size * depth,
-            bytes_accessed=count * (tile_size * depth * 2 + tile_size * tile_size * 4),
-            transcendentals=0,
-        ),
+        cost_estimate=took(TILE_COST * count),
         name=f"tiles_{count - 1}",
     )(where, *halves)
 
 
+class Reduction:
+    def __init__(self, members, order, keep, send):
+        self.members, self.order = members, order
+        self.keep, self.send = keep, send
+        self.step = 0
+
+    def advance(self):
+        if self.step < len(self.order):
+            bit = 1 << self.order[self.step]
+            came = lax.ppermute(
+                self.send, "aux", [(at, at ^ bit) for at in range(2 ** len(self.order))]
+            )
+            self.step += 1
+            if self.step < len(self.order):
+                middle = self.keep.shape[0] // 2
+                self.send = self.keep[middle:] + came[middle:]
+                self.keep = self.keep[:middle] + came[:middle]
+            else:
+                self.send = self.keep[:, 1] + came[:, 1]
+                self.keep = self.keep[:, 0] + came[:, 0]
+        elif self.step == len(self.order):
+            self.step += 1
+            self.keep = self.keep + lax.ppermute(self.send, "occ", [(0, 1), (1, 0)])
+            self.send = None
+
+
+def hold(value, reductions):
+    live = [one for one in reductions if one.send is not None]
+    value, sends = lax.optimization_barrier((value, [one.send for one in live]))
+    for one, send in zip(live, sends):
+        one.send = send
+    return value
+
+
 def slab_body(integrals, orbitals):
-    parts = lax.axis_size("aux")
-    bits = parts.bit_length() - 1
+    bits = lax.axis_size("aux").bit_length() - 1
     me = lax.axis_index("occ")
     count = integrals.shape[0] // 2
     where = jnp.stack(
@@ -248,26 +300,55 @@
     received = []
     for block in range(NB):
         sent = half_call(block, False, where, coeffs, integrals)
-        if block >= 2:
-            sent, received[-2] = lax.optimization_barrier((sent, received[-2]))
+        if block >= DEPTH:
+            sent, received[-DEPTH] = lax.optimization_barrier((sent, received[-DEPTH]))
         received.append(lax.ppermute(sent, "occ", swap))
-    halves, columns = [], []
+    halves, running = [], []
     for block in range(NB):
-        halves.append(half_call(block, True, where, coeffs, integrals, received[block]))
-        keep, send = tile_call(bits, where, halves)
-        for step in range(bits):
-            pairs = [(at, at ^ (1 << step)) for at in range(parts)]
-            came = lax.ppermute(send, "aux", pairs)
-            if step < bits - 1:
-                middle = keep.shape[0] // 2
-                send = keep[middle:] + came[middle:]
-                keep = keep[:middle] + came[:middle]
-            else:
-                send = keep[:, 1] + came[:, 1]
-                keep = keep[:, 0] + came[:, 0]
-        columns.append((keep + lax.ppermute(send, "occ", swap))[0])
-    order = [columns[high][low] for low in range(NB) for high in range(low, NB)]
-    return jnp.stack(order, axis=1)
+        for one in running:
+            one.advance()
+        half = half_call(block, True, where, coeffs, integrals, received[block])
+        halves.append(hold(half, running))
+        groups = tile_groups(block, bits)
+        parts = tile_call(groups, where, halves)
+        fresh = [
+            Reduction(members, order, *parts[2 * at : 2 * at + 2])
+            for at, (members, order) in enumerate(groups)
+        ]
+        if block < NB - 1:
+            running += fresh
+    for one in fresh:
+        one.advance()
+    for step in range(bits):
+        for one in running:
+            if one.step < bits:
+                one.advance()
+        fresh_sends, sends = lax.optimization_barrier(
+            ([one.send for one in fresh], [one.send for one in running if one.send is not None])
+        )
+        for one, send in zip(fresh, fresh_sends):
+            one.send = send
+        for one, send in zip([one for one in running if one.send is not None], sends):
+            one.send = send
+        for one in running + fresh:
+            if one.step < bits and one in fresh:
+                one.advance()
+    columns = {}
+    for one in running + fresh:
+        while one.send is not None:
+            one.advance()
+    at = 0
+    every = running + fresh
+    for block in range(NB):
+        seen = 0
+        while seen <= block:
+            for place, tile in enumerate(every[at].members):
+                columns[tile, block] = every[at].keep[0, place]
+                seen += 1
+            at += 1
+    return jnp.stack(
+        [columns[low, high] for low in range(NB) for high in range(low, NB)], axis=1
+    )
 
 
 def body(integrals, orbitals):

time: 389 us -> 340 us (0.87)
  waiting for transfers between devices: 203 us -> 164 us
  Pallas kernels: 112 us -> 105 us
  other arithmetic: 15.4 us -> 9.04 us
    ppermute x30 -> x35, waiting for transfers between devices: 126 us -> 96.8 us  [the longest x28 86.5 us: advance(): lax.ppermute(self.send, 'aux', [(at, at ^ bit) for at in range(2 ** len(s...]
    ppermute x6, waiting for transfers between devices: 77 us -> 67.1 us  [slab_body(): received.append(lax.ppermute(sent, 'occ', swap))]
    add x29 -> x34, other arithmetic: 15.3 us -> 8.95 us  [the longest x21 8.09 us: advance(): self.keep = self.keep[:middle] + came[:middle]]
    pallas_call x6, Pallas kernels: 29.1 us -> 23.4 us  [tile_call(): pl.pallas_call(functools.partial(tile_kernel, groups), out_shape=outs, in...]
    ppermute x30 -> x35, starting transfers between devices: 39.8 us -> 43 us  [the longest x28 34.9 us: advance(): lax.ppermute(self.send, 'aux', [(at, at ^ bit) for at in range(2 ** len(s...]
  transfers between devices with their start and end apart: 36 -> 41, of which waited for: 20 -> 22; matrix products, arithmetic and copies ran while one was open for 4% -> 2% of each run, Pallas kernels for 27% -> 29%
where the time goes in v2:
time: 340 us; the launch traced here: 339 us
  waiting for transfers between devices  164 us (48%)
  Pallas kernels  105 us (31%)
  starting transfers between devices  53.4 us (16%)
  other arithmetic  9.04 us (3%)
  local copies, waits for them, and re-layouts  7.06 us (2%)
    ppermute x28, waiting for transfers between devices, advance(): lax.ppermute(self.send, 'aux', [(at, at ^ bit) for at in range(2 ** len(s...  86.5 us
    pallas_call x12, Pallas kernels, half_call(): pl.pallas_call(functools.partial(half_kernel, block, owned), out_shape=ou...  81.5 us
    ppermute x6, waiting for transfers between devices, slab_body(): received.append(lax.ppermute(sent, 'occ', swap))  67.1 us
    ppermute x28, starting transfers between devices, advance(): lax.ppermute(self.send, 'aux', [(at, at ^ bit) for at in range(2 ** len(s...  34.9 us
    pallas_call x6, Pallas kernels, tile_call(): pl.pallas_call(functools.partial(tile_kernel, groups), out_shape=outs, in...  23.4 us
    ppermute x6, starting transfers between devices, slab_body(): received.append(lax.ppermute(sent, 'occ', swap))  10.3 us
    ppermute x7, waiting for transfers between devices, advance(): self.keep = self.keep + lax.ppermute(self.send, 'occ', [(0, 1), (1, 0)])  10.2 us
    ppermute x7, starting transfers between devices, advance(): self.keep = self.keep + lax.ppermute(self.send, 'occ', [(0, 1), (1, 0)])  8.12 us
  transfers between devices with their start and end apart: 41, of which 22 were waited for; matrix products, arithmetic and copies ran while one was open for 2% of the time, Pallas kernels for 29%

profile of v2, /device:TPU:0, one launch (start us, length us, event | category | flops | bytes accessed | tf_op | source)
XLA Modules:
  0.0 339.0 jit_solution(3759023976155290573)
XLA Ops:
  0.0 2.8 copy.3
  2.9 6.7 %half_send_0.1 = bf16[4,384,256]{2,1,0:T(8,128)(2,1)} custom-call(s32[4]{0:T(128)S(1)} %pad_add_fusion.where, bf16[384,3072]{1,0:T(8,128)(2,1)S(1)} %bitcast.135, bf16[8,21,256,512]{3,2,1,0:T(8,128)(2,1)} %refs_5_.23, bf16[8,21,256,512]{3,2,1,0:T(8,128)(2,1)} %refs_5_.23, bf16[8,21,256,512]{3,2,1,0:T(8,128)(2,1)} %refs_5_.23, ...), custom_call_target="tpu_custom_call" | custom-call | flops 1150000000 | bytes 1 | tf_op jit(solution)/shard_map/half_send_0/pallas_call | solution.py:178
  9.6 2.9 collective-permute-start
  12.5 7.0 %half_send_1.1 = bf16[4,384,512]{2,1,0:T(8,128)(2,1)} custom-call(s32[4]{0:T(128)S(1)} %pad_add_fusion.where, bf16[384,3072]{1,0:T(8,128)(2,1)S(1)} %bitcast.136, bf16[8,21,256,512]{3,2,1,0:T(8,128)(2,1)} %refs_5_.23, bf16[8,21,256,512]{3,2,1,0:T(8,128)(2,1)} %refs_5_.23, bf16[8,21,256,512]{3,2,1,0:T(8,128)(2,1)} %refs_5_.23, ...), custom_call_target="tpu_custom_call" | custom-call | flops 1150000000 | bytes 1 | tf_op jit(solution)/shard_map/half_send_1/pallas_call | solution.py:178
  19.6 7.0 %half_send_2.1 = bf16[4,384,512]{2,1,0:T(8,128)(2,1)} custom-call(s32[4]{0:T(128)S(1)} %pad_add_fusion.where, bf16[384,3072]{1,0:T(8,128)(2,1)S(1)} %bitcast.137, bf16[8,21,256,512]{3,2,1,0:T(8,128)(2,1)} %refs_5_.23, bf16[8,21,256,512]{3,2,1,0:T(8,128)(2,1)} %refs_5_.23, bf16[8,21,256,512]{3,2,1,0:T(8,128)(2,1)} %refs_5_.23, ...), custom_call_target="tpu_custom_call" | custom-call | flops 1150000000 | bytes 1 | tf_op jit(solution)/shard_map/half_send_2/pallas_call | solution.py:178
  26.6 4.6 %collective-permute-done.refs_6_ = bf16[4,384,256]{2,1,0:T(8,128)(2,1)} collective-permute-done((bf16[4,384,256]{2,1,0:T(8,128)(2,1)}, bf16[4,384,256]{2,1,0:T(8,128)(2,1)}, u32[]{:S(2)}, u32[]{:S(2)}) %collective-permute-start) | collective-permute-done | bytes 786464 | tf_op jit(solution)/shard_map/ppermute | solution.py:305
  31.2 6.7 %half_own_0.1.refs_0_ = bf16[512,1536]{1,0:T(8,128)(2,1)S(1)} custom-call(s32[4]{0:T(128)S(1)} %pad_add_fusion.where, bf16[384,3072]{1,0:T(8,128)(2,1)S(1)} %bitcast.138, bf16[8,21,256,512]{3,2,1,0:T(8,128)(2,1)} %refs_5_.23, bf16[8,21,256,512]{3,2,1,0:T(8,128)(2,1)} %refs_5_.23, bf16[8,21,256,512]{3,2,1,0:T(8,128)(2,1)} %refs_5_.23, ...), custom_call_target="tpu_custom_call" | custom-call | flops 23000000512 | bytes 1 | tf_op jit(solution)/shard_map/half_own_0/pallas_call | solution.py:178
  39.6 6.9 %half_send_3.1 = bf16[4,384,512]{2,1,0:T(8,128)(2,1)} custom-call(s32[4]{0:T(128)S(1)} %pad_add_fusion.where, bf16[384,3072]{1,0:T(8,128)(2,1)S(1)} %bitcast.139, bf16[8,21,256,512]{3,2,1,0:T(8,128)(2,1)} %refs_5_.23, bf16[8,21,256,512]{3,2,1,0:T(8,128)(2,1)} %refs_5_.23, bf16[8,21,256,512]{3,2,1,0:T(8,128)(2,1)} %refs_5_.23, ...), custom_call_target="tpu_custom_call" | custom-call | flops 1150000000 | bytes 1 | tf_op jit(solution)/shard_map/half_send_3/pallas_call | solution.py:178
  46.5 2.1 collective-permute-start.4
  49.4 15.5 %collective-permute-done.2.refs_6_ = bf16[4,384,512]{2,1,0:T(8,128)(2,1)} collective-permute-done((bf16[4,384,512]{2,1,0:T(8,128)(2,1)}, bf16[4,384,512]{2,1,0:T(8,128)(2,1)}, u32[]{:S(2)}, u32[]{:S(2)}) %collective-permute-start.2) | collective-permute-done | bytes 1572896 | tf_op jit(solution)/shard_map/ppermute | solution.py:305
  64.9 6.9 %half_own_1.1.refs_1_ = bf16[512,1536]{1,0:T(8,128)(2,1)S(1)} custom-call(s32[4]{0:T(128)S(1)} %pad_add_fusion.where, bf16[384,3072]{1,0:T(8,128)(2,1)S(1)} %bitcast.140, bf16[8,21,256,512]{3,2,1,0:T(8,128)(2,1)} %refs_5_.23, bf16[8,21,256,512]{3,2,1,0:T(8,128)(2,1)} %refs_5_.23, bf16[8,21,256,512]{3,2,1,0:T(8,128)(2,1)} %refs_5_.23, ...), custom_call_target="tpu_custom_call" | custom-call | flops 23000000512 | bytes 1 | tf_op jit(solution)/shard_map/half_own_1/pallas_call | solution.py:178
  71.8 2.2 collective-permute-start.3
  74.0 6.1 %half_send_4.1 = bf16[4,384,512]{2,1,0:T(8,128)(2,1)S(1)} custom-call(s32[4]{0:T(128)S(1)} %pad_add_fusion.where, bf16[384,3072]{1,0:T(8,128)(2,1)S(1)} %bitcast.141, bf16[8,21,256,512]{3,2,1,0:T(8,128)(2,1)} %refs_5_.23, bf16[8,21,256,512]{3,2,1,0:T(8,128)(2,1)} %refs_5_.23, bf16[8,21,256,512]{3,2,1,0:T(8,128)(2,1)} %refs_5_.23, ...), custom_call_target="tpu_custom_call" | custom-call | flops 1150000000 | bytes 1 | tf_op jit(solution)/shard_map/half_send_4/pallas_call | solution.py:178
  80.1 1.6 collective-permute-start.7
  81.7 2.5 tiles_1.1
  85.0 13.7 %collective-permute-done.4.refs_6_ = bf16[4,384,512]{2,1,0:T(8,128)(2,1)} collective-permute-done((bf16[4,384,512]{2,1,0:T(8,128)(2,1)}, bf16[4,384,512]{2,1,0:T(8,128)(2,1)}, u32[]{:S(2)}, u32[]{:S(2)}) %collective-permute-start.4) | collective-permute-done | bytes 1572896 | tf_op jit(solution)/shard_map/ppermute | solution.py:305
  98.6 6.9 %half_own_2.1.refs_2_ = bf16[512,1536]{1,0:T(8,128)(2,1)S(1)} custom-call(s32[4]{0:T(128)S(1)} %pad_add_fusion.where, bf16[384,3072]{1,0:T(8,128)(2,1)S(1)} %bitcast.142, bf16[8,21,256,512]{3,2,1,0:T(8,128)(2,1)} %refs_5_.23, bf16[8,21,256,512]{3,2,1,0:T(8,128)(2,1)} %refs_5_.23, bf16[8,21,256,512]{3,2,1,0:T(8,128)(2,1)} %refs_5_.23, ...), custom_call_target="tpu_custom_call" | custom-call | flops 23000000512 | bytes 1 | tf_op jit(solution)/shard_map/half_own_2/pallas_call | solution.py:178
  105.7 2.2 collective-permute-start.8
  109.5 7.0 %half_send_5.1 = bf16[4,384,512]{2,1,0:T(8,128)(2,1)} custom-call(s32[4]{0:T(128)S(1)} %pad_add_fusion.where, bf16[384,3072]{1,0:T(8,128)(2,1)S(1)} %bitcast.143, bf16[8,21,256,512]{3,2,1,0:T(8,128)(2,1)} %refs_5_.23, bf16[8,21,256,512]{3,2,1,0:T(8,128)(2,1)} %refs_5_.23, bf16[8,21,256,512]{3,2,1,0:T(8,128)(2,1)} %refs_5_.23, ...), custom_call_target="tpu_custom_call" | custom-call | flops 1150000000 | bytes 1 | tf_op jit(solution)/shard_map/half_send_5/pallas_call | solution.py:178
  118.0 3.3 tiles_2.1
  122.1 10.2 %collective-permute-done.7.refs_6_ = bf16[4,384,512]{2,1,0:T(8,128)(2,1)} collective-permute-done((bf16[4,384,512]{2,1,0:T(8,128)(2,1)}, bf16[4,384,512]{2,1,0:T(8,128)(2,1)}, u32[]{:S(2)}, u32[]{:S(2)}) %collective-permute-start.7) | collective-permute-done | bytes 1572896 | tf_op jit(solution)/shard_map/ppermute | solution.py:305
  132.3 2.1 collective-permute-start.17
  135.2 6.8 %half_own_3.1.refs_3_ = bf16[512,1536]{1,0:T(8,128)(2,1)S(1)} custom-call(s32[4]{0:T(128)S(1)} %pad_add_fusion.where, bf16[384,3072]{1,0:T(8,128)(2,1)S(1)} %bitcast.144, bf16[8,21,256,512]{3,2,1,0:T(8,128)(2,1)} %refs_5_.23, bf16[8,21,256,512]{3,2,1,0:T(8,128)(2,1)} %refs_5_.23, bf16[8,21,256,512]{3,2,1,0:T(8,128)(2,1)} %refs_5_.23, ...), custom_call_target="tpu_custom_call" | custom-call | flops 23000000512 | bytes 1 | tf_op jit(solution)/shard_map/half_own_3/pallas_call | solution.py:178
  142.3 2.7 collective-permute-start.10
  148.1 4.2 %tiles_3.1 = (f32[8,2,4,32,256]{4,3,2,1,0:T(8,128)S(1)}, f32[8,2,4,32,256]{4,3,2,1,0:T(8,128)S(1)}) custom-call(s32[4]{0:T(128)S(1)} %pad_add_fusion.where, bf16[512,1536]{1,0:T(8,128)(2,1)S(1)} %half_own_0.1.refs_0_, bf16[512,1536]{1,0:T(8,128)(2,1)S(1)} %copy-done.1, bf16[512,1536]{1,0:T(8,128)(2,1)S(1)} %half_own_2.1.refs_2_, ...), custom_call_target="tpu_custom_call" | custom-call | flops 460000000 | bytes 1 | tf_op jit(solution)/shard_map/tiles_3/pallas_call | solution.py:244
  152.3 13.7 %collective-permute-done.11.refs_6_ = bf16[4,384,512]{2,1,0:T(8,128)(2,1)S(1)} collective-permute-done((bf16[4,384,512]{2,1,0:T(8,128)(2,1)S(1)}, bf16[4,384,512]{2,1,0:T(8,128)(2,1)S(1)}, u32[]{:S(2)}, u32[]{:S(2)}) %collective-permute-start.11) | collective-permute-done | bytes 1572896 | tf_op jit(solution)/shard_map/ppermute | solution.py:305
  168.5 6.6 %half_own_4.1.refs_4_ = bf16[512,1536]{1,0:T(8,128)(2,1)S(1)} custom-call(s32[4]{0:T(128)S(1)} %pad_add_fusion.where, bf16[384,3072]{1,0:T(8,128)(2,1)S(1)} %bitcast.145, bf16[8,21,256,512]{3,2,1,0:T(8,128)(2,1)} %refs_5_.23, bf16[8,21,256,512]{3,2,1,0:T(8,128)(2,1)} %refs_5_.23, bf16[8,21,256,512]{3,2,1,0:T(8,128)(2,1)} %refs_5_.23, ...), custom_call_target="tpu_custom_call" | custom-call | flops 23000000512 | bytes 1 | tf_op jit(solution)/shard_map/half_own_4/pallas_call | solution.py:178
  178.1 3.2 collective-permute-start.16
  184.4 5.0 %tiles_4.1 = (f32[8,2,5,32,256]{4,3,2,1,0:T(8,128)S(1)}, f32[8,2,5,32,256]{4,3,2,1,0:T(8,128)S(1)}) custom-call(s32[4]{0:T(128)S(1)} %pad_add_fusion.where, bf16[512,1536]{1,0:T(8,128)(2,1)S(1)} %half_own_0.1.refs_0_, bf16[512,1536]{1,0:T(8,128)(2,1)S(1)} %copy-done.1, bf16[512,1536]{1,0:T(8,128)(2,1)S(1)} %half_own_2.1.refs_2_, ...), custom_call_target="tpu_custom_call" | custom-call | flops 575000000 | bytes 1 | tf_op jit(solution)/shard_map/tiles_4/pallas_call | solution.py:244
  189.5 9.4 %collective-permute-done.17.refs_6_ = bf16[4,384,512]{2,1,0:T(8,128)(2,1)} collective-permute-done((bf16[4,384,512]{2,1,0:T(8,128)(2,1)}, bf16[4,384,512]{2,1,0:T(8,128)(2,1)}, u32[]{:S(2)}, u32[]{:S(2)}) %collective-permute-start.17) | collective-permute-done | bytes 1572896 | tf_op jit(solution)/shard_map/ppermute | solution.py:305
  198.9 7.1 %half_own_5.1.refs_5_ = bf16[512,1536]{1,0:T(8,128)(2,1)S(1)} custom-call(s32[4]{0:T(128)S(1)} %pad_add_fusion.where, bf16[384,3072]{1,0:T(8,128)(2,1)S(1)} %bitcast.146, bf16[8,21,256,512]{3,2,1,0:T(8,128)(2,1)} %refs_5_.23, bf16[8,21,256,512]{3,2,1,0:T(8,128)(2,1)} %refs_5_.23, bf16[8,21,256,512]{3,2,1,0:T(8,128)(2,1)} %refs_5_.23, ...), custom_call_target="tpu_custom_call" | custom-call | flops 23000000512 | bytes 1 | tf_op jit(solution)/shard_map/half_own_5/pallas_call | solution.py:178
  206.1 2.0 collective-permute-done.19
  210.6 6.8 %tiles_5.1 = (f32[8,2,3,32,256]{4,3,2,1,0:T(8,128)S(1)}, f32[8,2,3,32,256]{4,3,2,1,0:T(8,128)S(1)}, f32[8,2,3,32,256]{4,3,2,1,0:T(8,128)S(1)}, f32[8,2,3,32,256]{4,3,2,1,0:T(8,128)S(1)}) custom-call(s32[4]{0:T(128)S(1)} %pad_add_fusion.where, bf16[512,1536]{1,0:T(8,128)(2,1)S(1)} %half_own_0.1.refs_0_, bf16[512,1536]{1,0:T(8,128)(2,1)S(1)} %copy-done.1, ...), custom_call_target="tpu_custom_call" | custom-call | flops 690000000 | bytes 1 | tf_op jit(solution)/shard_map/tiles_5/pallas_call | solution.py:244
  218.7 2.6 collective-permute-start.23
  221.3 13.0 %collective-permute-done.23 = f32[1,2,3,32,256]{4,3,2,1,0:T(8,128)S(1)} collective-permute-done((f32[1,2,3,32,256]{4,3,2,1,0:T(8,128)S(1)}, f32[1,2,3,32,256]{4,3,2,1,0:T(8,128)S(1)}, u32[]{:S(2)}, u32[]{:S(2)}) %collective-permute-start.23) | collective-permute-done | bytes 196640 | tf_op jit(solution)/shard_map/ppermute | solution.py:266
  234.4 1.7 collective-permute-done.24
  236.2 2.7 collective-permute-done.25
  242.0 2.6 collective-permute-start.28
  245.0 16.2 %collective-permute-done.28 = f32[1,2,4,32,256]{4,3,2,1,0:T(8,128)S(1)} collective-permute-done((f32[1,2,4,32,256]{4,3,2,1,0:T(8,128)S(1)}, f32[1,2,4,32,256]{4,3,2,1,0:T(8,128)S(1)}, u32[]{:S(2)}, u32[]{:S(2)}) %collective-permute-start.28) | collective-permute-done | bytes 262176 | tf_op jit(solution)/shard_map/ppermute | solution.py:266
  263.0 14.2 %collective-permute-done.27 = f32[4,2,3,32,256]{4,3,2,1,0:T(8,128)S(1)} collective-permute-done((f32[4,2,3,32,256]{4,3,2,1,0:T(8,128)S(1)}, f32[4,2,3,32,256]{4,3,2,1,0:T(8,128)S(1)}, u32[]{:S(2)}, u32[]{:S(2)}) %collective-permute-start.27) | collective-permute-done | bytes 786464 | tf_op jit(solution)/shard_map/ppermute | solution.py:266
  280.7 13.9 %collective-permute-done.32 = f32[1,2,5,32,256]{4,3,2,1,0:T(8,128)S(1)} collective-permute-done((f32[1,2,5,32,256]{4,3,2,1,0:T(8,128)S(1)}, f32[1,2,5,32,256]{4,3,2,1,0:T(8,128)S(1)}, u32[]{:S(2)}, u32[]{:S(2)}) %collective-permute-start.32) | collective-permute-done | bytes 327712 | tf_op jit(solution)/shard_map/ppermute | solution.py:266
  295.5 13.8 %collective-permute-done.31 = f32[2,2,3,32,256]{4,3,2,1,0:T(8,128)S(1)} collective-permute-done((f32[2,2,3,32,256]{4,3,2,1,0:T(8,128)S(1)}, f32[2,2,3,32,256]{4,3,2,1,0:T(8,128)S(1)}, u32[]{:S(2)}, u32[]{:S(2)}) %collective-permute-start.31) | collective-permute-done | bytes 393248 | tf_op jit(solution)/shard_map/ppermute | solution.py:266
  311.0 2.5 collective-permute-start.34
  313.6 6.7 %collective-permute-done.33 = f32[1,2,3,32,256]{4,3,2,1,0:T(8,128)S(1)} collective-permute-done((f32[1,2,3,32,256]{4,3,2,1,0:T(8,128)S(1)}, f32[1,2,3,32,256]{4,3,2,1,0:T(8,128)S(1)}, u32[]{:S(2)}, u32[]{:S(2)}) %collective-permute-start.33) | collective-permute-done | bytes 196640 | tf_op jit(solution)/shard_map/ppermute | solution.py:266
  327.7 2.1 collective-permute-done.39
  329.8 2.1 collective-permute-done.40
  331.9 2.8 collective-permute-done.37
  334.8 2.5 collective-permute-done.38
  (141 shorter events, 44.8 us)
Async XLA Ops:
  9.6 21.6 %collective-permute-start = (bf16[4,384,256]{2,1,0:T(8,128)(2,1)}, bf16[4,384,256]{2,1,0:T(8,128)(2,1)}, u32[]{:S(2)}, u32[]{:S(2)}) collective-permute-start(bf16[4,384,256]{2,1,0:T(8,128)(2,1)} %half_send_0.1), channel_id=1, source_target_pairs={{0,1},{1,0},{2,3},{3,2},{4,5},{5,4},{6,7},{7,6},{8,9},{9,8},{10,11... | collective-permute-start | bytes 2359304 | tf_op jit(solution)/shard_map/ppermute | solution.py:305
  19.6 45.4 %collective-permute-start.2 = (bf16[4,384,512]{2,1,0:T(8,128)(2,1)}, bf16[4,384,512]{2,1,0:T(8,128)(2,1)}, u32[]{:S(2)}, u32[]{:S(2)}) collective-permute-start(bf16[4,384,512]{2,1,0:T(8,128)(2,1)} %half_send_1.1), channel_id=1, source_target_pairs={{0,1},{1,0},{2,3},{3,2},{4,5},{5,4},{6,7},{7,6},{8,9},{9,8},{10,11... | collective-permute-start | bytes 4718600 | tf_op jit(solution)/shard_map/ppermute | solution.py:305
  39.5 9.1 %collective-permute-start.1 = (f32[8,2,1,32,256]{4,3,2,1,0:T(8,128)S(1)}, f32[8,2,1,32,256]{4,3,2,1,0:T(8,128)S(1)}, u32[]{:S(2)}, u32[]{:S(2)}) collective-permute-start(f32[8,2,1,32,256]{4,3,2,1,0:T(8,128)S(1)} %get-tuple-element.72), channel_id=1, source_target_pairs={{0,2},{2,0},{4,6},{6,4},{8,10},{10,8},{12,14},{14,12},{16,18},{18,... | collective-permute-start | bytes 1572872 | tf_op jit(solution)/shard_map/ppermute | solution.py:266
  46.5 52.1 %collective-permute-start.4 = (bf16[4,384,512]{2,1,0:T(8,128)(2,1)}, bf16[4,384,512]{2,1,0:T(8,128)(2,1)}, u32[]{:S(2)}, u32[]{:S(2)}) collective-permute-start(bf16[4,384,512]{2,1,0:T(8,128)(2,1)} %half_send_2.1), channel_id=1, source_target_pairs={{0,1},{1,0},{2,3},{3,2},{4,5},{5,4},{6,7},{7,6},{8,9},{9,8},{10,11... | collective-permute-start | bytes 4718600 | tf_op jit(solution)/shard_map/ppermute | solution.py:305
  71.8 9.9 %copy-start = (bf16[512,1536]{1,0:T(8,128)(2,1)}, bf16[512,1536]{1,0:T(8,128)(2,1)S(1)}, u32[]{:S(2)}) copy-start(bf16[512,1536]{1,0:T(8,128)(2,1)S(1)} %half_own_1.1.refs_1_) | copy-start | bytes 4718596
  71.8 12.4 %collective-permute-start.3 = (f32[4,2,1,32,256]{4,3,2,1,0:T(8,128)S(1)}, f32[4,2,1,32,256]{4,3,2,1,0:T(8,128)S(1)}, u32[]{:S(2)}, u32[]{:S(2)}) collective-permute-start(f32[4,2,1,32,256]{4,3,2,1,0:T(8,128)S(1)} %get-tuple-element.74), channel_id=1, source_target_pairs={{0,4},{2,6},{4,0},{6,2},{8,12},{10,14},{12,8},{14,10},{16,20},{18,... | collective-permute-start | bytes 786440 | tf_op jit(solution)/shard_map/ppermute | solution.py:266
  80.1 52.3 %collective-permute-start.7 = (bf16[4,384,512]{2,1,0:T(8,128)(2,1)}, bf16[4,384,512]{2,1,0:T(8,128)(2,1)}, u32[]{:S(2)}, u32[]{:S(2)}) collective-permute-start(bf16[4,384,512]{2,1,0:T(8,128)(2,1)} %half_send_3.1), channel_id=1, source_target_pairs={{0,1},{1,0},{2,3},{3,2},{4,5},{5,4},{6,7},{7,6},{8,9},{9,8},{10,11... | collective-permute-start | bytes 4718600 | tf_op jit(solution)/shard_map/ppermute | solution.py:305
  84.2 21.3 %collective-permute-start.5 = (f32[8,2,2,32,256]{4,3,2,1,0:T(8,128)S(1)}, f32[8,2,2,32,256]{4,3,2,1,0:T(8,128)S(1)}, u32[]{:S(2)}, u32[]{:S(2)}) collective-permute-start(f32[8,2,2,32,256]{4,3,2,1,0:T(8,128)S(1)} %get-tuple-element.79), channel_id=1, source_target_pairs={{0,2},{2,0},{4,6},{6,4},{8,10},{10,8},{12,14},{14,12},{16,18},{18,... | collective-permute-start | bytes 3145736 | tf_op jit(solution)/shard_map/ppermute | solution.py:266
  105.7 12.3 %copy-start.1 = (bf16[512,1536]{1,0:T(8,128)(2,1)S(1)}, bf16[512,1536]{1,0:T(8,128)(2,1)}, u32[]{:S(2)}) copy-start(bf16[512,1536]{1,0:T(8,128)(2,1)} %copy-done) | copy-start | bytes 4718596
  105.7 28.7 %collective-permute-start.8 = (f32[4,2,2,32,256]{4,3,2,1,0:T(8,128)S(1)}, f32[4,2,2,32,256]{4,3,2,1,0:T(8,128)S(1)}, u32[]{:S(2)}, u32[]{:S(2)}) collective-permute-start(f32[4,2,2,32,256]{4,3,2,1,0:T(8,128)S(1)} %get-tuple-element.83), channel_id=1, source_target_pairs={{0,4},{2,6},{4,0},{6,2},{8,12},{10,14},{12,8},{14,10},{16,20},{18,... | collective-permute-start | bytes 1572872 | tf_op jit(solution)/shard_map/ppermute | solution.py:266
  107.9 13.5 %collective-permute-start.6 = (f32[2,2,1,32,256]{4,3,2,1,0:T(8,128)S(1)}, f32[2,2,1,32,256]{4,3,2,1,0:T(8,128)S(1)}, u32[]{:S(2)}, u32[]{:S(2)}) collective-permute-start(f32[2,2,1,32,256]{4,3,2,1,0:T(8,128)S(1)} %get-tuple-element.80), channel_id=1, source_target_pairs={{0,8},{2,10},{4,12},{6,14},{8,0},{10,2},{12,4},{14,6},{16,24},{18,... | collective-permute-start | bytes 393224 | tf_op jit(solution)/shard_map/ppermute | solution.py:266
  116.4 49.5 %collective-permute-start.11 = (bf16[4,384,512]{2,1,0:T(8,128)(2,1)S(1)}, bf16[4,384,512]{2,1,0:T(8,128)(2,1)S(1)}, u32[]{:S(2)}, u32[]{:S(2)}) collective-permute-start(bf16[4,384,512]{2,1,0:T(8,128)(2,1)S(1)} %half_send_4.1), channel_id=1, source_target_pairs={{0,1},{1,0},{2,3},{3,2},{4,5},{5,4},{6,7},{7,6},{8,9},{9,8},{10,11... | collective-permute-start | bytes 4718600 | tf_op jit(solution)/shard_map/ppermute | solution.py:305
  121.3 20.6 %collective-permute-start.9 = (f32[8,2,3,32,256]{4,3,2,1,0:T(8,128)S(1)}, f32[8,2,3,32,256]{4,3,2,1,0:T(8,128)S(1)}, u32[]{:S(2)}, u32[]{:S(2)}) collective-permute-start(f32[8,2,3,32,256]{4,3,2,1,0:T(8,128)S(1)} %get-tuple-element.86), channel_id=1, source_target_pairs={{0,2},{2,0},{4,6},{6,4},{8,10},{10,8},{12,14},{14,12},{16,18},{18,... | collective-permute-start | bytes 4718600 | tf_op jit(solution)/shard_map/ppermute | solution.py:266
  132.3 66.6 %collective-permute-start.17 = (bf16[4,384,512]{2,1,0:T(8,128)(2,1)}, bf16[4,384,512]{2,1,0:T(8,128)(2,1)}, u32[]{:S(2)}, u32[]{:S(2)}) collective-permute-start(bf16[4,384,512]{2,1,0:T(8,128)(2,1)} %half_send_5.1), channel_id=1, source_target_pairs={{0,1},{1,0},{2,3},{3,2},{4,5},{5,4},{6,7},{7,6},{8,9},{9,8},{10,11... | collective-permute-start | bytes 4718600 | tf_op jit(solution)/shard_map/ppermute | solution.py:305
  142.3 32.8 %collective-permute-start.10 = (f32[1,2,1,32,256]{4,3,2,1,0:T(8,128)S(1)}, f32[1,2,1,32,256]{4,3,2,1,0:T(8,128)S(1)}, u32[]{:S(2)}, u32[]{:S(2)}) collective-permute-start(f32[1,2,1,32,256]{4,3,2,1,0:T(8,128)S(1)} %get-tuple-element.87), channel_id=1, source_target_pairs={{0,16},{2,18},{4,20},{6,22},{8,24},{10,26},{12,28},{14,30},{16,0},... | collective-permute-start | bytes 196616 | tf_op jit(solution)/shard_map/ppermute | solution.py:266
  145.0 30.8 %collective-permute-start.12 = (f32[2,2,2,32,256]{4,3,2,1,0:T(8,128)S(1)}, f32[2,2,2,32,256]{4,3,2,1,0:T(8,128)S(1)}, u32[]{:S(2)}, u32[]{:S(2)}) collective-permute-start(f32[2,2,2,32,256]{4,3,2,1,0:T(8,128)S(1)} %get-tuple-element.89), channel_id=1, source_target_pairs={{0,8},{2,10},{4,12},{6,14},{8,0},{10,2},{12,4},{14,6},{16,24},{18,... | collective-permute-start | bytes 786440 | tf_op jit(solution)/shard_map/ppermute | solution.py:266
  146.5 29.3 %collective-permute-start.13 = (f32[4,2,3,32,256]{4,3,2,1,0:T(8,128)S(1)}, f32[4,2,3,32,256]{4,3,2,1,0:T(8,128)S(1)}, u32[]{:S(2)}, u32[]{:S(2)}) collective-permute-start(f32[4,2,3,32,256]{4,3,2,1,0:T(8,128)S(1)} %get-tuple-element.90), channel_id=1, source_target_pairs={{0,4},{2,6},{4,0},{6,2},{8,12},{10,14},{12,8},{14,10},{16,20},{18,... | collective-permute-start | bytes 2359304 | tf_op jit(solution)/shard_map/ppermute | solution.py:266
  167.1 9.6 %collective-permute-start.14 = (f32[8,2,4,32,256]{4,3,2,1,0:T(8,128)S(1)}, f32[8,2,4,32,256]{4,3,2,1,0:T(8,128)S(1)}, u32[]{:S(2)}, u32[]{:S(2)}) collective-permute-start(f32[8,2,4,32,256]{4,3,2,1,0:T(8,128)S(1)} %get-tuple-element.93), channel_id=1, source_target_pairs={{0,2},{2,0},{4,6},{6,4},{8,10},{10,8},{12,14},{14,12},{16,18},{18,... | collective-permute-start | bytes 6291464 | tf_op jit(solution)/shard_map/ppermute | solution.py:266
  168.5 7.2 %copy-start.5 = (f32[2,2,2,32,256]{4,3,2,1,0:T(8,128)S(1)}, f32[2,2,2,32,256]{4,3,2,1,0:T(8,128)}, u32[]{:S(2)}) copy-start(f32[2,2,2,32,256]{4,3,2,1,0:T(8,128)} %get-tuple-element.161) | copy-start | bytes 786436
  178.1 27.8 %collective-permute-start.16 = (f32[1,2,2,32,256]{4,3,2,1,0:T(8,128)S(1)}, f32[1,2,2,32,256]{4,3,2,1,0:T(8,128)S(1)}, u32[]{:S(2)}, u32[]{:S(2)}) collective-permute-start(f32[1,2,2,32,256]{4,3,2,1,0:T(8,128)S(1)} %get-tuple-element.95), channel_id=1, source_target_pairs={{0,16},{2,18},{4,20},{6,22},{8,24},{10,26},{12,28},{14,30},{16,0},... | collective-permute-start | bytes 393224 | tf_op jit(solution)/shard_map/ppermute | solution.py:266
  181.3 24.7 %collective-permute-start.18 = (f32[2,2,3,32,256]{4,3,2,1,0:T(8,128)}, f32[2,2,3,32,256]{4,3,2,1,0:T(8,128)S(1)}, u32[]{:S(2)}, u32[]{:S(2)}) collective-permute-start(f32[2,2,3,32,256]{4,3,2,1,0:T(8,128)} %get-tuple-element.98), channel_id=1, source_target_pairs={{0,8},{2,10},{4,12},{6,14},{8,0},{10,2},{12,4},{14,6},{16,24},{18,... | collective-permute-start | bytes 1179656 | tf_op jit(solution)/shard_map/ppermute | solution.py:266
  182.9 25.2 %collective-permute-start.19 = (f32[4,2,4,32,256]{4,3,2,1,0:T(8,128)}, f32[4,2,4,32,256]{4,3,2,1,0:T(8,128)S(1)}, u32[]{:S(2)}, u32[]{:S(2)}) collective-permute-start(f32[4,2,4,32,256]{4,3,2,1,0:T(8,128)} %get-tuple-element.99), channel_id=1, source_target_pairs={{0,4},{2,6},{4,0},{6,2},{8,12},{10,14},{12,8},{14,10},{16,20},{18,... | collective-permute-start | bytes 3145736 | tf_op jit(solution)/shard_map/ppermute | solution.py:266
  189.4 18.8 %collective-permute-start.20 = (f32[8,2,5,32,256]{4,3,2,1,0:T(8,128)S(1)}, f32[8,2,5,32,256]{4,3,2,1,0:T(8,128)S(1)}, u32[]{:S(2)}, u32[]{:S(2)}) collective-permute-start(f32[8,2,5,32,256]{4,3,2,1,0:T(8,128)S(1)} %get-tuple-element.101), channel_id=1, source_target_pairs={{0,2},{2,0},{4,6},{6,4},{8,10},{10,8},{12,14},{14,12},{16,18},{18,... | collective-permute-start | bytes 7864328 | tf_op jit(solution)/shard_map/ppermute | solution.py:266
  209.0 29.8 %collective-permute-start.25 = (f32[4,2,5,32,256]{4,3,2,1,0:T(8,128)S(1)}, f32[4,2,5,32,256]{4,3,2,1,0:T(8,128)S(1)}, u32[]{:S(2)}, u32[]{:S(2)}) collective-permute-start(f32[4,2,5,32,256]{4,3,2,1,0:T(8,128)S(1)} %get-tuple-element.110), channel_id=1, source_target_pairs={{0,4},{2,6},{4,0},{6,2},{8,12},{10,14},{12,8},{14,10},{16,20},{18,... | collective-permute-start | bytes 3932168 | tf_op jit(solution)/shard_map/ppermute | solution.py:266
  217.4 21.7 %collective-permute-start.21 = (f32[8,2,3,32,256]{4,3,2,1,0:T(8,128)S(1)}, f32[8,2,3,32,256]{4,3,2,1,0:T(8,128)S(1)}, u32[]{:S(2)}, u32[]{:S(2)}) collective-permute-start(f32[8,2,3,32,256]{4,3,2,1,0:T(8,128)S(1)} %get-tuple-element.104), channel_id=1, source_target_pairs={{0,2},{2,0},{4,6},{6,4},{8,10},{10,8},{12,14},{14,12},{16,18},{18,... | collective-permute-start | bytes 4718600 | tf_op jit(solution)/shard_map/ppermute | solution.py:266
  217.5 22.0 %collective-permute-start.22 = (f32[8,2,3,32,256]{4,3,2,1,0:T(8,128)S(1)}, f32[8,2,3,32,256]{4,3,2,1,0:T(8,128)S(1)}, u32[]{:S(2)}, u32[]{:S(2)}) collective-permute-start(f32[8,2,3,32,256]{4,3,2,1,0:T(8,128)S(1)} %get-tuple-element.106), channel_id=1, source_target_pairs={{0,2},{2,0},{4,6},{6,4},{8,10},{10,8},{12,14},{14,12},{16,18},{18,... | collective-permute-start | bytes 4718600 | tf_op jit(solution)/shard_map/ppermute | solution.py:266
  218.0 18.1 %collective-permute-start.24 = (f32[2,2,4,32,256]{4,3,2,1,0:T(8,128)S(1)}, f32[2,2,4,32,256]{4,3,2,1,0:T(8,128)S(1)}, u32[]{:S(2)}, u32[]{:S(2)}) collective-permute-start(f32[2,2,4,32,256]{4,3,2,1,0:T(8,128)S(1)} %get-tuple-element.109), channel_id=1, source_target_pairs={{0,8},{2,10},{4,12},{6,14},{8,0},{10,2},{12,4},{14,6},{16,24},{18,... | collective-permute-start | bytes 1572872 | tf_op jit(solution)/shard_map/ppermute | solution.py:266
  218.7 15.6 %collective-permute-start.23 = (f32[1,2,3,32,256]{4,3,2,1,0:T(8,128)S(1)}, f32[1,2,3,32,256]{4,3,2,1,0:T(8,128)S(1)}, u32[]{:S(2)}, u32[]{:S(2)}) collective-permute-start(f32[1,2,3,32,256]{4,3,2,1,0:T(8,128)S(1)} %get-tuple-element.108), channel_id=1, source_target_pairs={{0,16},{2,18},{4,20},{6,22},{8,24},{10,26},{12,28},{14,30},{16,0},... | collective-permute-start | bytes 589832 | tf_op jit(solution)/shard_map/ppermute | solution.py:266
  239.8 23.0 %collective-permute-start.29 = (f32[2,2,5,32,256]{4,3,2,1,0:T(8,128)S(1)}, f32[2,2,5,32,256]{4,3,2,1,0:T(8,128)S(1)}, u32[]{:S(2)}, u32[]{:S(2)}) collective-permute-start(f32[2,2,5,32,256]{4,3,2,1,0:T(8,128)S(1)} %get-tuple-element.116), channel_id=1, source_target_pairs={{0,8},{2,10},{4,12},{6,14},{8,0},{10,2},{12,4},{14,6},{16,24},{18,... | collective-permute-start | bytes 1966088 | tf_op jit(solution)/shard_map/ppermute | solution.py:266
  240.5 22.4 %collective-permute-start.26 = (f32[4,2,3,32,256]{4,3,2,1,0:T(8,128)S(1)}, f32[4,2,3,32,256]{4,3,2,1,0:T(8,128)S(1)}, u32[]{:S(2)}, u32[]{:S(2)}) collective-permute-start(f32[4,2,3,32,256]{4,3,2,1,0:T(8,128)S(1)} %get-tuple-element.111), channel_id=1, source_target_pairs={{0,4},{2,6},{4,0},{6,2},{8,12},{10,14},{12,8},{14,10},{16,20},{18,... | collective-permute-start | bytes 2359304 | tf_op jit(solution)/shard_map/ppermute | solution.py:266
  242.0 19.3 %collective-permute-start.28 = (f32[1,2,4,32,256]{4,3,2,1,0:T(8,128)S(1)}, f32[1,2,4,32,256]{4,3,2,1,0:T(8,128)S(1)}, u32[]{:S(2)}, u32[]{:S(2)}) collective-permute-start(f32[1,2,4,32,256]{4,3,2,1,0:T(8,128)S(1)} %get-tuple-element.115), channel_id=1, source_target_pairs={{0,16},{2,18},{4,20},{6,22},{8,24},{10,26},{12,28},{14,30},{16,0},... | collective-permute-start | bytes 786440 | tf_op jit(solution)/shard_map/ppermute | solution.py:266
  244.6 32.6 %collective-permute-start.27 = (f32[4,2,3,32,256]{4,3,2,1,0:T(8,128)S(1)}, f32[4,2,3,32,256]{4,3,2,1,0:T(8,128)S(1)}, u32[]{:S(2)}, u32[]{:S(2)}) collective-permute-start(f32[4,2,3,32,256]{4,3,2,1,0:T(8,128)S(1)} %get-tuple-element.112), channel_id=1, source_target_pairs={{0,8},{2,10},{4,12},{6,14},{8,0},{10,2},{12,4},{14,6},{16,24},{18,... | collective-permute-start | bytes 2359304 | tf_op jit(solution)/shard_map/ppermute | solution.py:266
  277.3 32.2 %copy-start.14 = (f32[1,1,32,256]{3,2,1,0:T(8,128)S(1)}, f32[1,1,32,256]{3,2,1,0:T(8,128)}, u32[]{:S(2)}) copy-start(f32[1,1,32,256]{3,2,1,0:T(8,128)} %fusion.18) | copy-start | bytes 98308
  277.3 17.3 %collective-permute-start.32 = (f32[1,2,5,32,256]{4,3,2,1,0:T(8,128)S(1)}, f32[1,2,5,32,256]{4,3,2,1,0:T(8,128)S(1)}, u32[]{:S(2)}, u32[]{:S(2)}) collective-permute-start(f32[1,2,5,32,256]{4,3,2,1,0:T(8,128)S(1)} %get-tuple-element.122), channel_id=1, source_target_pairs={{0,16},{2,18},{4,20},{6,22},{8,24},{10,26},{12,28},{14,30},{16,0},... | collective-permute-start | bytes 983048 | tf_op jit(solution)/shard_map/ppermute | solution.py:266
  278.8 16.6 %collective-permute-start.30 = (f32[2,2,3,32,256]{4,3,2,1,0:T(8,128)S(1)}, f32[2,2,3,32,256]{4,3,2,1,0:T(8,128)S(1)}, u32[]{:S(2)}, u32[]{:S(2)}) collective-permute-start(f32[2,2,3,32,256]{4,3,2,1,0:T(8,128)S(1)} %get-tuple-element.117), channel_id=1, source_target_pairs={{0,8},{2,10},{4,12},{6,14},{8,0},{10,2},{12,4},{14,6},{16,24},{18,... | collective-permute-start | bytes 1179656 | tf_op jit(solution)/shard_map/ppermute | solution.py:266
  280.4 28.9 %collective-permute-start.31 = (f32[2,2,3,32,256]{4,3,2,1,0:T(8,128)S(1)}, f32[2,2,3,32,256]{4,3,2,1,0:T(8,128)S(1)}, u32[]{:S(2)}, u32[]{:S(2)}) collective-permute-start(f32[2,2,3,32,256]{4,3,2,1,0:T(8,128)S(1)} %get-tuple-element.118), channel_id=1, source_target_pairs={{0,16},{2,18},{4,20},{6,22},{8,24},{10,26},{12,28},{14,30},{16,0},... | collective-permute-start | bytes 1179656 | tf_op jit(solution)/shard_map/ppermute | solution.py:266
  294.6 27.3 %copy-start.9 = (f32[1,2,1,32,256]{4,3,2,1,0:T(8,128)S(1)}, f32[1,2,1,32,256]{4,3,2,1,0:T(8,128)}, u32[]{:S(2)}) copy-start(f32[1,2,1,32,256]{4,3,2,1,0:T(8,128)} %get-tuple-element.175) | copy-start | bytes 196612
  294.6 27.3 %copy-start.13 = (f32[1,2,1,32,256]{4,3,2,1,0:T(8,128)S(1)}, f32[1,2,1,32,256]{4,3,2,1,0:T(8,128)}, u32[]{:S(2)}) copy-start(f32[1,2,1,32,256]{4,3,2,1,0:T(8,128)} %copy-done.12) | copy-start | bytes 196612
  294.6 32.2 %copy-start.11 = (f32[1,2,2,32,256]{4,3,2,1,0:T(8,128)S(1)}, f32[1,2,2,32,256]{4,3,2,1,0:T(8,128)}, u32[]{:S(2)}) copy-start(f32[1,2,2,32,256]{4,3,2,1,0:T(8,128)} %copy-done.10) | copy-start | bytes 393220
  309.3 10.9 %collective-permute-start.33 = (f32[1,2,3,32,256]{4,3,2,1,0:T(8,128)S(1)}, f32[1,2,3,32,256]{4,3,2,1,0:T(8,128)S(1)}, u32[]{:S(2)}, u32[]{:S(2)}) collective-permute-start(f32[1,2,3,32,256]{4,3,2,1,0:T(8,128)S(1)} %get-tuple-element.123), channel_id=1, source_target_pairs={{0,16},{2,18},{4,20},{6,22},{8,24},{10,26},{12,28},{14,30},{16,0},... | collective-permute-start | bytes 589832 | tf_op jit(solution)/shard_map/ppermute | solution.py:266
  309.4 12.5 %collective-permute-start.15 = (f32[1,1,32,256]{3,2,1,0:T(8,128)S(1)}, f32[1,1,32,256]{3,2,1,0:T(8,128)S(1)}, u32[]{:S(2)}, u32[]{:S(2)}) collective-permute-start(f32[1,1,32,256]{3,2,1,0:T(8,128)S(1)} %copy-done.14), channel_id=1, source_target_pairs={{0,1},{1,0},{2,3},{3,2},{4,5},{5,4},{6,7},{7,6},{8,9},{9,8},{10,11... | collective-permute-start | bytes 98312 | tf_op jit(solution)/shard_map/ppermute | solution.py:279
  311.0 9.2 %collective-permute-start.34 = (f32[1,2,3,32,256]{4,3,2,1,0:T(8,128)S(1)}, f32[1,2,3,32,256]{4,3,2,1,0:T(8,128)S(1)}, u32[]{:S(2)}, u32[]{:S(2)}) collective-permute-start(f32[1,2,3,32,256]{4,3,2,1,0:T(8,128)S(1)} %get-tuple-element.124), channel_id=1, source_target_pairs={{0,4},{2,6},{4,0},{6,2},{8,12},{10,14},{12,8},{14,10},{16,20},{18,... | collective-permute-start | bytes 589832 | tf_op jit(solution)/shard_map/ppermute | solution.py:266
  320.3 5.8 %collective-permute-start.35 = (f32[1,2,32,256]{3,2,1,0:T(8,128)S(1)}, f32[1,2,32,256]{3,2,1,0:T(8,128)S(1)}, u32[]{:S(2)}, u32[]{:S(2)}) collective-permute-start(f32[1,2,32,256]{3,2,1,0:T(8,128)S(1)} %fusion.15), channel_id=1, source_target_pairs={{0,1},{1,0},{2,3},{3,2},{4,5},{5,4},{6,7},{7,6},{8,9},{9,8},{10,11... | collective-permute-start | bytes 196616 | tf_op jit(solution)/shard_map/ppermute | solution.py:279
  321.9 5.8 %collective-permute-start.36 = (f32[1,3,32,256]{3,2,1,0:T(8,128)S(1)}, f32[1,3,32,256]{3,2,1,0:T(8,128)S(1)}, u32[]{:S(2)}, u32[]{:S(2)}) collective-permute-start(f32[1,3,32,256]{3,2,1,0:T(8,128)S(1)} %fusion.14), channel_id=1, source_target_pairs={{0,1},{1,0},{2,3},{3,2},{4,5},{5,4},{6,7},{7,6},{8,9},{9,8},{10,11... | collective-permute-start | bytes 294920 | tf_op jit(solution)/shard_map/ppermute | solution.py:279
  322.5 7.3 %collective-permute-start.39 = (f32[1,3,32,256]{3,2,1,0:T(8,128)S(1)}, f32[1,3,32,256]{3,2,1,0:T(8,128)S(1)}, u32[]{:S(2)}, u32[]{:S(2)}) collective-permute-start(f32[1,3,32,256]{3,2,1,0:T(8,128)S(1)} %fusion.13), channel_id=1, source_target_pairs={{0,1},{1,0},{2,3},{3,2},{4,5},{5,4},{6,7},{7,6},{8,9},{9,8},{10,11... | collective-permute-start | bytes 294920 | tf_op jit(solution)/shard_map/ppermute | solution.py:279
  324.0 7.9 %collective-permute-start.40 = (f32[1,3,32,256]{3,2,1,0:T(8,128)S(1)}, f32[1,3,32,256]{3,2,1,0:T(8,128)S(1)}, u32[]{:S(2)}, u32[]{:S(2)}) collective-permute-start(f32[1,3,32,256]{3,2,1,0:T(8,128)S(1)} %fusion.12), channel_id=1, source_target_pairs={{0,1},{1,0},{2,3},{3,2},{4,5},{5,4},{6,7},{7,6},{8,9},{9,8},{10,11... | collective-permute-start | bytes 294920 | tf_op jit(solution)/shard_map/ppermute | solution.py:279
  324.5 10.2 %collective-permute-start.37 = (f32[1,4,32,256]{3,2,1,0:T(8,128)S(1)}, f32[1,4,32,256]{3,2,1,0:T(8,128)S(1)}, u32[]{:S(2)}, u32[]{:S(2)}) collective-permute-start(f32[1,4,32,256]{3,2,1,0:T(8,128)S(1)} %fusion.5), channel_id=1, source_target_pairs={{0,1},{1,0},{2,3},{3,2},{4,5},{5,4},{6,7},{7,6},{8,9},{9,8},{10,11... | collective-permute-start | bytes 393224 | tf_op jit(solution)/shard_map/ppermute | solution.py:279
  326.1 11.2 %collective-permute-start.38 = (f32[1,5,32,256]{3,2,1,0:T(8,128)S(1)}, f32[1,5,32,256]{3,2,1,0:T(8,128)S(1)}, u32[]{:S(2)}, u32[]{:S(2)}) collective-permute-start(f32[1,5,32,256]{3,2,1,0:T(8,128)S(1)} %fusion.2), channel_id=1, source_target_pairs={{0,1},{1,0},{2,3},{3,2},{4,5},{5,4},{6,7},{7,6},{8,9},{9,8},{10,11... | collective-permute-start | bytes 491528 | tf_op jit(solution)/shard_map/ppermute | solution.py:279
  (9 other events, 24.5 us)

commit v3 on v2

--- a/solution.py
+++ b/solution.py
@@ -195,9 +195,8 @@
     plain = tuple(range(bits))
     if block < NB - 1 or bits < 3:
         return [(tuple(range(block + 1)), plain)]
-    turned = (0,) + tuple(range(2, bits)) + (1,)
     middle = (block + 1) // 2
-    return [(tuple(range(middle)), plain), (tuple(range(middle, block + 1)), turned)]
+    return [(tuple(range(middle)), plain), (tuple(range(middle, block + 1)), plain)]
 
 
 def relative_owner(place, order):
@@ -319,20 +318,25 @@
             running += fresh
     for one in fresh:
         one.advance()
-    for step in range(bits):
+    for _ in range(bits):
         for one in running:
+            if one.send is not None:
+                one.advance()
+        fresh_sends, held = lax.optimization_barrier(
+            (
+                [one.send for one in fresh],
+                [one.keep if one.send is None else one.send for one in running],
+            )
+        )
+        for one, send in zip(fresh, fresh_sends):
+            one.send = send
             if one.step < bits:
                 one.advance()
-        fresh_sends, sends = lax.optimization_barrier(
-            ([one.send for one in fresh], [one.send for one in running if one.send is not None])
-        )
-        for one, send in zip(fresh, fresh_sends):
-            one.send = send
-        for one, send in zip([one for one in running if one.send is not None], sends):
-            one.send = send
-        for one in running + fresh:
-            if one.step < bits and one in fresh:
-                one.advance()
+        for one, value in zip(running, held):
+            if one.send is None:
+                one.keep = value
+            else:
+                one.send = value
     columns = {}
     for one in running + fresh:
         while one.send is not None:

time: 340 us -> 328 us (0.965)
  waiting for transfers between devices: 164 us -> 152 us
    ppermute x28, waiting for transfers between devices: 86.5 us -> 77 us  [advance(): lax.ppermute(self.send, 'aux', [(at, at ^ bit) for at in range(2 ** len(s...]
  transfers between devices with their start and end apart: 41 -> 41, of which waited for: 22 -> 24; matrix products, arithmetic and copies ran while one was open for 2% -> 2% of each run, Pallas kernels for 29% -> 30%
where the time goes in v3:
time: 328 us; the launch traced here: 327 us
  waiting for transfers between devices  152 us (46%)
  Pallas kernels  105 us (32%)
  starting transfers between devices  52.8 us (16%)
  other arithmetic  9.05 us (3%)
  local copies, waits for them, and re-layouts  7.06 us (2%)
    pallas_call x12, Pallas kernels, half_call(): pl.pallas_call(functools.partial(half_kernel, block, owned), out_shape=ou...  81.5 us
    ppermute x28, waiting for transfers between devices, advance(): lax.ppermute(self.send, 'aux', [(at, at ^ bit) for at in range(2 ** len(s...  77 us
    ppermute x6, waiting for transfers between devices, slab_body(): received.append(lax.ppermute(sent, 'occ', swap))  67.1 us
    ppermute x28, starting transfers between devices, advance(): lax.ppermute(self.send, 'aux', [(at, at ^ bit) for at in range(2 ** len(s...  34.7 us
    pallas_call x6, Pallas kernels, tile_call(): pl.pallas_call(functools.partial(tile_kernel, groups), out_shape=outs, in...  23.4 us
    ppermute x6, starting transfers between devices, slab_body(): received.append(lax.ppermute(sent, 'occ', swap))  10.3 us
    ppermute x7, waiting for transfers between devices, advance(): self.keep = self.keep + lax.ppermute(self.send, 'occ', [(0, 1), (1, 0)])  8.31 us
    add x21, other arithmetic, advance(): self.keep = self.keep[:middle] + came[:middle]  8.11 us
  transfers between devices with their start and end apart: 41, of which 24 were waited for; matrix products, arithmetic and copies ran while one was open for 2% of the time, Pallas kernels for 30%

profile of v3, /device:TPU:0, one launch (start us, length us, event | category | flops | bytes accessed | tf_op | source)
XLA Modules:
  0.0 326.9 jit_solution(15199935480451416458)
XLA Ops:
  0.0 2.8 copy.3
  2.9 6.7 %half_send_0.1 = bf16[4,384,256]{2,1,0:T(8,128)(2,1)} custom-call(s32[4]{0:T(128)S(1)} %pad_add_fusion.where, bf16[384,3072]{1,0:T(8,128)(2,1)S(1)} %bitcast.101, bf16[8,21,256,512]{3,2,1,0:T(8,128)(2,1)} %refs_5_.23, bf16[8,21,256,512]{3,2,1,0:T(8,128)(2,1)} %refs_5_.23, bf16[8,21,256,512]{3,2,1,0:T(8,128)(2,1)} %refs_5_.23, ...), custom_call_target="tpu_custom_call" | custom-call | flops 1150000000 | bytes 1 | tf_op jit(solution)/shard_map/half_send_0/pallas_call | solution.py:178
  9.6 2.9 collective-permute-start
  12.5 7.0 %half_send_1.1 = bf16[4,384,512]{2,1,0:T(8,128)(2,1)} custom-call(s32[4]{0:T(128)S(1)} %pad_add_fusion.where, bf16[384,3072]{1,0:T(8,128)(2,1)S(1)} %bitcast.102, bf16[8,21,256,512]{3,2,1,0:T(8,128)(2,1)} %refs_5_.23, bf16[8,21,256,512]{3,2,1,0:T(8,128)(2,1)} %refs_5_.23, bf16[8,21,256,512]{3,2,1,0:T(8,128)(2,1)} %refs_5_.23, ...), custom_call_target="tpu_custom_call" | custom-call | flops 1150000000 | bytes 1 | tf_op jit(solution)/shard_map/half_send_1/pallas_call | solution.py:178
  19.6 7.0 %half_send_2.1 = bf16[4,384,512]{2,1,0:T(8,128)(2,1)} custom-call(s32[4]{0:T(128)S(1)} %pad_add_fusion.where, bf16[384,3072]{1,0:T(8,128)(2,1)S(1)} %bitcast.103, bf16[8,21,256,512]{3,2,1,0:T(8,128)(2,1)} %refs_5_.23, bf16[8,21,256,512]{3,2,1,0:T(8,128)(2,1)} %refs_5_.23, bf16[8,21,256,512]{3,2,1,0:T(8,128)(2,1)} %refs_5_.23, ...), custom_call_target="tpu_custom_call" | custom-call | flops 1150000000 | bytes 1 | tf_op jit(solution)/shard_map/half_send_2/pallas_call | solution.py:178
  26.6 4.6 %collective-permute-done.refs_6_ = bf16[4,384,256]{2,1,0:T(8,128)(2,1)} collective-permute-done((bf16[4,384,256]{2,1,0:T(8,128)(2,1)}, bf16[4,384,256]{2,1,0:T(8,128)(2,1)}, u32[]{:S(2)}, u32[]{:S(2)}) %collective-permute-start) | collective-permute-done | bytes 786464 | tf_op jit(solution)/shard_map/ppermute | solution.py:304
  31.2 6.7 %half_own_0.1.refs_0_ = bf16[512,1536]{1,0:T(8,128)(2,1)S(1)} custom-call(s32[4]{0:T(128)S(1)} %pad_add_fusion.where, bf16[384,3072]{1,0:T(8,128)(2,1)S(1)} %bitcast.104, bf16[8,21,256,512]{3,2,1,0:T(8,128)(2,1)} %refs_5_.23, bf16[8,21,256,512]{3,2,1,0:T(8,128)(2,1)} %refs_5_.23, bf16[8,21,256,512]{3,2,1,0:T(8,128)(2,1)} %refs_5_.23, ...), custom_call_target="tpu_custom_call" | custom-call | flops 23000000512 | bytes 1 | tf_op jit(solution)/shard_map/half_own_0/pallas_call | solution.py:178
  39.6 6.9 %half_send_3.1 = bf16[4,384,512]{2,1,0:T(8,128)(2,1)} custom-call(s32[4]{0:T(128)S(1)} %pad_add_fusion.where, bf16[384,3072]{1,0:T(8,128)(2,1)S(1)} %bitcast.105, bf16[8,21,256,512]{3,2,1,0:T(8,128)(2,1)} %refs_5_.23, bf16[8,21,256,512]{3,2,1,0:T(8,128)(2,1)} %refs_5_.23, bf16[8,21,256,512]{3,2,1,0:T(8,128)(2,1)} %refs_5_.23, ...), custom_call_target="tpu_custom_call" | custom-call | flops 1150000000 | bytes 1 | tf_op jit(solution)/shard_map/half_send_3/pallas_call | solution.py:178
  46.5 2.1 collective-permute-start.3
  49.4 15.5 %collective-permute-done.1.refs_6_ = bf16[4,384,512]{2,1,0:T(8,128)(2,1)} collective-permute-done((bf16[4,384,512]{2,1,0:T(8,128)(2,1)}, bf16[4,384,512]{2,1,0:T(8,128)(2,1)}, u32[]{:S(2)}, u32[]{:S(2)}) %collective-permute-start.1) | collective-permute-done | bytes 1572896 | tf_op jit(solution)/shard_map/ppermute | solution.py:304
  64.9 6.9 %half_own_1.1.refs_1_ = bf16[512,1536]{1,0:T(8,128)(2,1)S(1)} custom-call(s32[4]{0:T(128)S(1)} %pad_add_fusion.where, bf16[384,3072]{1,0:T(8,128)(2,1)S(1)} %bitcast.106, bf16[8,21,256,512]{3,2,1,0:T(8,128)(2,1)} %refs_5_.23, bf16[8,21,256,512]{3,2,1,0:T(8,128)(2,1)} %refs_5_.23, bf16[8,21,256,512]{3,2,1,0:T(8,128)(2,1)} %refs_5_.23, ...), custom_call_target="tpu_custom_call" | custom-call | flops 23000000512 | bytes 1 | tf_op jit(solution)/shard_map/half_own_1/pallas_call | solution.py:178
  71.8 2.2 collective-permute-start.4
  74.0 6.1 %half_send_4.1 = bf16[4,384,512]{2,1,0:T(8,128)(2,1)S(1)} custom-call(s32[4]{0:T(128)S(1)} %pad_add_fusion.where, bf16[384,3072]{1,0:T(8,128)(2,1)S(1)} %bitcast.107, bf16[8,21,256,512]{3,2,1,0:T(8,128)(2,1)} %refs_5_.23, bf16[8,21,256,512]{3,2,1,0:T(8,128)(2,1)} %refs_5_.23, bf16[8,21,256,512]{3,2,1,0:T(8,128)(2,1)} %refs_5_.23, ...), custom_call_target="tpu_custom_call" | custom-call | flops 1150000000 | bytes 1 | tf_op jit(solution)/shard_map/half_send_4/pallas_call | solution.py:178
  81.7 2.5 tiles_1.1
  85.0 13.7 %collective-permute-done.3.refs_6_ = bf16[4,384,512]{2,1,0:T(8,128)(2,1)} collective-permute-done((bf16[4,384,512]{2,1,0:T(8,128)(2,1)}, bf16[4,384,512]{2,1,0:T(8,128)(2,1)}, u32[]{:S(2)}, u32[]{:S(2)}) %collective-permute-start.3) | collective-permute-done | bytes 1572896 | tf_op jit(solution)/shard_map/ppermute | solution.py:304
  98.6 6.9 %half_own_2.1.refs_2_ = bf16[512,1536]{1,0:T(8,128)(2,1)S(1)} custom-call(s32[4]{0:T(128)S(1)} %pad_add_fusion.where, bf16[384,3072]{1,0:T(8,128)(2,1)S(1)} %bitcast.108, bf16[8,21,256,512]{3,2,1,0:T(8,128)(2,1)} %refs_5_.23, bf16[8,21,256,512]{3,2,1,0:T(8,128)(2,1)} %refs_5_.23, bf16[8,21,256,512]{3,2,1,0:T(8,128)(2,1)} %refs_5_.23, ...), custom_call_target="tpu_custom_call" | custom-call | flops 23000000512 | bytes 1 | tf_op jit(solution)/shard_map/half_own_2/pallas_call | solution.py:178
  105.7 2.2 collective-permute-start.8
  109.5 7.0 %half_send_5.1 = bf16[4,384,512]{2,1,0:T(8,128)(2,1)} custom-call(s32[4]{0:T(128)S(1)} %pad_add_fusion.where, bf16[384,3072]{1,0:T(8,128)(2,1)S(1)} %bitcast.109, bf16[8,21,256,512]{3,2,1,0:T(8,128)(2,1)} %refs_5_.23, bf16[8,21,256,512]{3,2,1,0:T(8,128)(2,1)} %refs_5_.23, bf16[8,21,256,512]{3,2,1,0:T(8,128)(2,1)} %refs_5_.23, ...), custom_call_target="tpu_custom_call" | custom-call | flops 1150000000 | bytes 1 | tf_op jit(solution)/shard_map/half_send_5/pallas_call | solution.py:178
  118.0 3.3 %tiles_2.1 = (f32[8,2,3,32,256]{4,3,2,1,0:T(8,128)S(1)}, f32[8,2,3,32,256]{4,3,2,1,0:T(8,128)S(1)}) custom-call(s32[4]{0:T(128)S(1)} %pad_add_fusion.where, bf16[512,1536]{1,0:T(8,128)(2,1)S(1)} %half_own_0.1.refs_0_, bf16[512,1536]{1,0:T(8,128)(2,1)S(1)} %copy-done.1, bf16[512,1536]{1,0:T(8,128)(2,1)S(1)} %half_own_2.1.refs_2_), custom_call_target="tpu_custom_call" | custom-call | flops 345000000 | bytes 1 | tf_op jit(solution)/shard_map/tiles_2/pallas_call | solution.py:243
  122.1 10.2 %collective-permute-done.6.refs_6_ = bf16[4,384,512]{2,1,0:T(8,128)(2,1)} collective-permute-done((bf16[4,384,512]{2,1,0:T(8,128)(2,1)}, bf16[4,384,512]{2,1,0:T(8,128)(2,1)}, u32[]{:S(2)}, u32[]{:S(2)}) %collective-permute-start.6) | collective-permute-done | bytes 1572896 | tf_op jit(solution)/shard_map/ppermute | solution.py:304
  132.3 2.1 collective-permute-start.15
  135.2 6.8 %half_own_3.1.refs_3_ = bf16[512,1536]{1,0:T(8,128)(2,1)S(1)} custom-call(s32[4]{0:T(128)S(1)} %pad_add_fusion.where, bf16[384,3072]{1,0:T(8,128)(2,1)S(1)} %bitcast.110, bf16[8,21,256,512]{3,2,1,0:T(8,128)(2,1)} %refs_5_.23, bf16[8,21,256,512]{3,2,1,0:T(8,128)(2,1)} %refs_5_.23, bf16[8,21,256,512]{3,2,1,0:T(8,128)(2,1)} %refs_5_.23, ...), custom_call_target="tpu_custom_call" | custom-call | flops 23000000512 | bytes 1 | tf_op jit(solution)/shard_map/half_own_3/pallas_call | solution.py:178
  142.3 2.7 collective-permute-start.11
  148.1 4.2 %tiles_3.1 = (f32[8,2,4,32,256]{4,3,2,1,0:T(8,128)S(1)}, f32[8,2,4,32,256]{4,3,2,1,0:T(8,128)S(1)}) custom-call(s32[4]{0:T(128)S(1)} %pad_add_fusion.where, bf16[512,1536]{1,0:T(8,128)(2,1)S(1)} %half_own_0.1.refs_0_, bf16[512,1536]{1,0:T(8,128)(2,1)S(1)} %copy-done.1, bf16[512,1536]{1,0:T(8,128)(2,1)S(1)} %half_own_2.1.refs_2_, ...), custom_call_target="tpu_custom_call" | custom-call | flops 460000000 | bytes 1 | tf_op jit(solution)/shard_map/tiles_3/pallas_call | solution.py:243
  152.3 13.7 %collective-permute-done.10.refs_6_ = bf16[4,384,512]{2,1,0:T(8,128)(2,1)S(1)} collective-permute-done((bf16[4,384,512]{2,1,0:T(8,128)(2,1)S(1)}, bf16[4,384,512]{2,1,0:T(8,128)(2,1)S(1)}, u32[]{:S(2)}, u32[]{:S(2)}) %collective-permute-start.10) | collective-permute-done | bytes 1572896 | tf_op jit(solution)/shard_map/ppermute | solution.py:304
  168.5 6.6 %half_own_4.1.refs_4_ = bf16[512,1536]{1,0:T(8,128)(2,1)S(1)} custom-call(s32[4]{0:T(128)S(1)} %pad_add_fusion.where, bf16[384,3072]{1,0:T(8,128)(2,1)S(1)} %bitcast.111, bf16[8,21,256,512]{3,2,1,0:T(8,128)(2,1)} %refs_5_.23, bf16[8,21,256,512]{3,2,1,0:T(8,128)(2,1)} %refs_5_.23, bf16[8,21,256,512]{3,2,1,0:T(8,128)(2,1)} %refs_5_.23, ...), custom_call_target="tpu_custom_call" | custom-call | flops 23000000512 | bytes 1 | tf_op jit(solution)/shard_map/half_own_4/pallas_call | solution.py:178
  178.1 3.2 collective-permute-start.16
  184.4 5.0 %tiles_4.1 = (f32[8,2,5,32,256]{4,3,2,1,0:T(8,128)S(1)}, f32[8,2,5,32,256]{4,3,2,1,0:T(8,128)S(1)}) custom-call(s32[4]{0:T(128)S(1)} %pad_add_fusion.where, bf16[512,1536]{1,0:T(8,128)(2,1)S(1)} %half_own_0.1.refs_0_, bf16[512,1536]{1,0:T(8,128)(2,1)S(1)} %copy-done.1, bf16[512,1536]{1,0:T(8,128)(2,1)S(1)} %half_own_2.1.refs_2_, ...), custom_call_target="tpu_custom_call" | custom-call | flops 575000000 | bytes 1 | tf_op jit(solution)/shard_map/tiles_4/pallas_call | solution.py:243
  189.5 9.4 %collective-permute-done.15.refs_6_ = bf16[4,384,512]{2,1,0:T(8,128)(2,1)} collective-permute-done((bf16[4,384,512]{2,1,0:T(8,128)(2,1)}, bf16[4,384,512]{2,1,0:T(8,128)(2,1)}, u32[]{:S(2)}, u32[]{:S(2)}) %collective-permute-start.15) | collective-permute-done | bytes 1572896 | tf_op jit(solution)/shard_map/ppermute | solution.py:304
  198.9 7.1 %half_own_5.1.refs_5_ = bf16[512,1536]{1,0:T(8,128)(2,1)S(1)} custom-call(s32[4]{0:T(128)S(1)} %pad_add_fusion.where, bf16[384,3072]{1,0:T(8,128)(2,1)S(1)} %bitcast.112, bf16[8,21,256,512]{3,2,1,0:T(8,128)(2,1)} %refs_5_.23, bf16[8,21,256,512]{3,2,1,0:T(8,128)(2,1)} %refs_5_.23, bf16[8,21,256,512]{3,2,1,0:T(8,128)(2,1)} %refs_5_.23, ...), custom_call_target="tpu_custom_call" | custom-call | flops 23000000512 | bytes 1 | tf_op jit(solution)/shard_map/half_own_5/pallas_call | solution.py:178
  206.1 2.0 collective-permute-done.18
  210.7 6.8 %tiles_5.1 = (f32[8,2,3,32,256]{4,3,2,1,0:T(8,128)S(1)}, f32[8,2,3,32,256]{4,3,2,1,0:T(8,128)S(1)}, f32[8,2,3,32,256]{4,3,2,1,0:T(8,128)S(1)}, f32[8,2,3,32,256]{4,3,2,1,0:T(8,128)S(1)}) custom-call(s32[4]{0:T(128)S(1)} %pad_add_fusion.where, bf16[512,1536]{1,0:T(8,128)(2,1)S(1)} %half_own_0.1.refs_0_, bf16[512,1536]{1,0:T(8,128)(2,1)S(1)} %copy-done.1, ...), custom_call_target="tpu_custom_call" | custom-call | flops 690000000 | bytes 1 | tf_op jit(solution)/shard_map/tiles_5/pallas_call | solution.py:243
  220.1 1.9 collective-permute-done.22
  223.8 1.8 collective-permute-start.24
  225.6 11.8 %collective-permute-done.24 = f32[1,2,3,32,256]{4,3,2,1,0:T(8,128)S(1)} collective-permute-done((f32[1,2,3,32,256]{4,3,2,1,0:T(8,128)S(1)}, f32[1,2,3,32,256]{4,3,2,1,0:T(8,128)S(1)}, u32[]{:S(2)}, u32[]{:S(2)}) %collective-permute-start.24) | collective-permute-done | bytes 196640 | tf_op jit(solution)/shard_map/ppermute | solution.py:265
  237.5 1.7 collective-permute-done.25
  240.3 1.8 collective-permute-start.31
  244.2 2.0 collective-permute-start.30
  247.3 12.9 %collective-permute-done.30 = f32[1,2,4,32,256]{4,3,2,1,0:T(8,128)S(1)} collective-permute-done((f32[1,2,4,32,256]{4,3,2,1,0:T(8,128)S(1)}, f32[1,2,4,32,256]{4,3,2,1,0:T(8,128)S(1)}, u32[]{:S(2)}, u32[]{:S(2)}) %collective-permute-start.30) | collective-permute-done | bytes 262176 | tf_op jit(solution)/shard_map/ppermute | solution.py:265
  261.0 3.1 collective-permute-done.27
  264.2 13.3 %collective-permute-done.28 = f32[4,2,3,32,256]{4,3,2,1,0:T(8,128)S(1)} collective-permute-done((f32[4,2,3,32,256]{4,3,2,1,0:T(8,128)S(1)}, f32[4,2,3,32,256]{4,3,2,1,0:T(8,128)S(1)}, u32[]{:S(2)}, u32[]{:S(2)}) %collective-permute-start.28) | collective-permute-done | bytes 786464 | tf_op jit(solution)/shard_map/ppermute | solution.py:265
  282.7 9.7 %collective-permute-done.35 = f32[1,2,5,32,256]{4,3,2,1,0:T(8,128)S(1)} collective-permute-done((f32[1,2,5,32,256]{4,3,2,1,0:T(8,128)S(1)}, f32[1,2,5,32,256]{4,3,2,1,0:T(8,128)S(1)}, u32[]{:S(2)}, u32[]{:S(2)}) %collective-permute-start.35) | collective-permute-done | bytes 327712 | tf_op jit(solution)/shard_map/ppermute | solution.py:265
  292.4 5.3 %collective-permute-done.32 = f32[2,2,3,32,256]{4,3,2,1,0:T(8,128)S(1)} collective-permute-done((f32[2,2,3,32,256]{4,3,2,1,0:T(8,128)S(1)}, f32[2,2,3,32,256]{4,3,2,1,0:T(8,128)S(1)}, u32[]{:S(2)}, u32[]{:S(2)}) %collective-permute-start.32) | collective-permute-done | bytes 393248 | tf_op jit(solution)/shard_map/ppermute | solution.py:265
  297.7 4.8 %collective-permute-done.33 = f32[2,2,3,32,256]{4,3,2,1,0:T(8,128)S(1)} collective-permute-done((f32[2,2,3,32,256]{4,3,2,1,0:T(8,128)S(1)}, f32[2,2,3,32,256]{4,3,2,1,0:T(8,128)S(1)}, u32[]{:S(2)}, u32[]{:S(2)}) %collective-permute-start.33) | collective-permute-done | bytes 393248 | tf_op jit(solution)/shard_map/ppermute | solution.py:265
  304.1 2.8 collective-permute-start.37
  308.1 8.9 %collective-permute-done.36 = f32[1,2,3,32,256]{4,3,2,1,0:T(8,128)S(1)} collective-permute-done((f32[1,2,3,32,256]{4,3,2,1,0:T(8,128)S(1)}, f32[1,2,3,32,256]{4,3,2,1,0:T(8,128)S(1)}, u32[]{:S(2)}, u32[]{:S(2)}) %collective-permute-start.36) | collective-permute-done | bytes 196640 | tf_op jit(solution)/shard_map/ppermute | solution.py:265
  317.0 2.7 collective-permute-done.37
  321.8 2.5 collective-permute-done.39
  (142 shorter events, 46.7 us)
Async XLA Ops:
  9.6 21.6 %collective-permute-start = (bf16[4,384,256]{2,1,0:T(8,128)(2,1)}, bf16[4,384,256]{2,1,0:T(8,128)(2,1)}, u32[]{:S(2)}, u32[]{:S(2)}) collective-permute-start(bf16[4,384,256]{2,1,0:T(8,128)(2,1)} %half_send_0.1), channel_id=1, source_target_pairs={{0,1},{1,0},{2,3},{3,2},{4,5},{5,4},{6,7},{7,6},{8,9},{9,8},{10,11... | collective-permute-start | bytes 2359304 | tf_op jit(solution)/shard_map/ppermute | solution.py:304
  19.6 45.4 %collective-permute-start.1 = (bf16[4,384,512]{2,1,0:T(8,128)(2,1)}, bf16[4,384,512]{2,1,0:T(8,128)(2,1)}, u32[]{:S(2)}, u32[]{:S(2)}) collective-permute-start(bf16[4,384,512]{2,1,0:T(8,128)(2,1)} %half_send_1.1), channel_id=1, source_target_pairs={{0,1},{1,0},{2,3},{3,2},{4,5},{5,4},{6,7},{7,6},{8,9},{9,8},{10,11... | collective-permute-start | bytes 4718600 | tf_op jit(solution)/shard_map/ppermute | solution.py:304
  39.5 9.1 %collective-permute-start.2 = (f32[8,2,1,32,256]{4,3,2,1,0:T(8,128)S(1)}, f32[8,2,1,32,256]{4,3,2,1,0:T(8,128)S(1)}, u32[]{:S(2)}, u32[]{:S(2)}) collective-permute-start(f32[8,2,1,32,256]{4,3,2,1,0:T(8,128)S(1)} %get-tuple-element.77), channel_id=1, source_target_pairs={{0,2},{2,0},{4,6},{6,4},{8,10},{10,8},{12,14},{14,12},{16,18},{18,... | collective-permute-start | bytes 1572872 | tf_op jit(solution)/shard_map/ppermute | solution.py:265
  46.5 52.1 %collective-permute-start.3 = (bf16[4,384,512]{2,1,0:T(8,128)(2,1)}, bf16[4,384,512]{2,1,0:T(8,128)(2,1)}, u32[]{:S(2)}, u32[]{:S(2)}) collective-permute-start(bf16[4,384,512]{2,1,0:T(8,128)(2,1)} %half_send_2.1), channel_id=1, source_target_pairs={{0,1},{1,0},{2,3},{3,2},{4,5},{5,4},{6,7},{7,6},{8,9},{9,8},{10,11... | collective-permute-start | bytes 4718600 | tf_op jit(solution)/shard_map/ppermute | solution.py:304
  71.8 9.9 %copy-start = (bf16[512,1536]{1,0:T(8,128)(2,1)}, bf16[512,1536]{1,0:T(8,128)(2,1)S(1)}, u32[]{:S(2)}) copy-start(bf16[512,1536]{1,0:T(8,128)(2,1)S(1)} %half_own_1.1.refs_1_) | copy-start | bytes 4718596
  71.8 12.4 %collective-permute-start.4 = (f32[4,2,1,32,256]{4,3,2,1,0:T(8,128)S(1)}, f32[4,2,1,32,256]{4,3,2,1,0:T(8,128)S(1)}, u32[]{:S(2)}, u32[]{:S(2)}) collective-permute-start(f32[4,2,1,32,256]{4,3,2,1,0:T(8,128)S(1)} %get-tuple-element.81), channel_id=1, source_target_pairs={{0,4},{2,6},{4,0},{6,2},{8,12},{10,14},{12,8},{14,10},{16,20},{18,... | collective-permute-start | bytes 786440 | tf_op jit(solution)/shard_map/ppermute | solution.py:265
  80.1 52.3 %collective-permute-start.6 = (bf16[4,384,512]{2,1,0:T(8,128)(2,1)}, bf16[4,384,512]{2,1,0:T(8,128)(2,1)}, u32[]{:S(2)}, u32[]{:S(2)}) collective-permute-start(bf16[4,384,512]{2,1,0:T(8,128)(2,1)} %half_send_3.1), channel_id=1, source_target_pairs={{0,1},{1,0},{2,3},{3,2},{4,5},{5,4},{6,7},{7,6},{8,9},{9,8},{10,11... | collective-permute-start | bytes 4718600 | tf_op jit(solution)/shard_map/ppermute | solution.py:304
  84.2 21.3 %collective-permute-start.5 = (f32[8,2,2,32,256]{4,3,2,1,0:T(8,128)S(1)}, f32[8,2,2,32,256]{4,3,2,1,0:T(8,128)S(1)}, u32[]{:S(2)}, u32[]{:S(2)}) collective-permute-start(f32[8,2,2,32,256]{4,3,2,1,0:T(8,128)S(1)} %get-tuple-element.83), channel_id=1, source_target_pairs={{0,2},{2,0},{4,6},{6,4},{8,10},{10,8},{12,14},{14,12},{16,18},{18,... | collective-permute-start | bytes 3145736 | tf_op jit(solution)/shard_map/ppermute | solution.py:265
  105.7 12.3 %copy-start.1 = (bf16[512,1536]{1,0:T(8,128)(2,1)S(1)}, bf16[512,1536]{1,0:T(8,128)(2,1)}, u32[]{:S(2)}) copy-start(bf16[512,1536]{1,0:T(8,128)(2,1)} %copy-done) | copy-start | bytes 4718596
  105.7 28.7 %collective-permute-start.8 = (f32[4,2,2,32,256]{4,3,2,1,0:T(8,128)S(1)}, f32[4,2,2,32,256]{4,3,2,1,0:T(8,128)S(1)}, u32[]{:S(2)}, u32[]{:S(2)}) collective-permute-start(f32[4,2,2,32,256]{4,3,2,1,0:T(8,128)S(1)} %get-tuple-element.88), channel_id=1, source_target_pairs={{0,4},{2,6},{4,0},{6,2},{8,12},{10,14},{12,8},{14,10},{16,20},{18,... | collective-permute-start | bytes 1572872 | tf_op jit(solution)/shard_map/ppermute | solution.py:265
  107.9 13.5 %collective-permute-start.7 = (f32[2,2,1,32,256]{4,3,2,1,0:T(8,128)S(1)}, f32[2,2,1,32,256]{4,3,2,1,0:T(8,128)S(1)}, u32[]{:S(2)}, u32[]{:S(2)}) collective-permute-start(f32[2,2,1,32,256]{4,3,2,1,0:T(8,128)S(1)} %get-tuple-element.87), channel_id=1, source_target_pairs={{0,8},{2,10},{4,12},{6,14},{8,0},{10,2},{12,4},{14,6},{16,24},{18,... | collective-permute-start | bytes 393224 | tf_op jit(solution)/shard_map/ppermute | solution.py:265
  116.4 49.5 %collective-permute-start.10 = (bf16[4,384,512]{2,1,0:T(8,128)(2,1)S(1)}, bf16[4,384,512]{2,1,0:T(8,128)(2,1)S(1)}, u32[]{:S(2)}, u32[]{:S(2)}) collective-permute-start(bf16[4,384,512]{2,1,0:T(8,128)(2,1)S(1)} %half_send_4.1), channel_id=1, source_target_pairs={{0,1},{1,0},{2,3},{3,2},{4,5},{5,4},{6,7},{7,6},{8,9},{9,8},{10,11... | collective-permute-start | bytes 4718600 | tf_op jit(solution)/shard_map/ppermute | solution.py:304
  121.3 20.6 %collective-permute-start.9 = (f32[8,2,3,32,256]{4,3,2,1,0:T(8,128)S(1)}, f32[8,2,3,32,256]{4,3,2,1,0:T(8,128)S(1)}, u32[]{:S(2)}, u32[]{:S(2)}) collective-permute-start(f32[8,2,3,32,256]{4,3,2,1,0:T(8,128)S(1)} %get-tuple-element.90), channel_id=1, source_target_pairs={{0,2},{2,0},{4,6},{6,4},{8,10},{10,8},{12,14},{14,12},{16,18},{18,... | collective-permute-start | bytes 4718600 | tf_op jit(solution)/shard_map/ppermute | solution.py:265
  132.3 66.6 %collective-permute-start.15 = (bf16[4,384,512]{2,1,0:T(8,128)(2,1)}, bf16[4,384,512]{2,1,0:T(8,128)(2,1)}, u32[]{:S(2)}, u32[]{:S(2)}) collective-permute-start(bf16[4,384,512]{2,1,0:T(8,128)(2,1)} %half_send_5.1), channel_id=1, source_target_pairs={{0,1},{1,0},{2,3},{3,2},{4,5},{5,4},{6,7},{7,6},{8,9},{9,8},{10,11... | collective-permute-start | bytes 4718600 | tf_op jit(solution)/shard_map/ppermute | solution.py:304
  142.3 32.8 %collective-permute-start.11 = (f32[1,2,1,32,256]{4,3,2,1,0:T(8,128)S(1)}, f32[1,2,1,32,256]{4,3,2,1,0:T(8,128)S(1)}, u32[]{:S(2)}, u32[]{:S(2)}) collective-permute-start(f32[1,2,1,32,256]{4,3,2,1,0:T(8,128)S(1)} %get-tuple-element.93), channel_id=1, source_target_pairs={{0,16},{2,18},{4,20},{6,22},{8,24},{10,26},{12,28},{14,30},{16,0},... | collective-permute-start | bytes 196616 | tf_op jit(solution)/shard_map/ppermute | solution.py:265
  145.0 30.8 %collective-permute-start.12 = (f32[2,2,2,32,256]{4,3,2,1,0:T(8,128)S(1)}, f32[2,2,2,32,256]{4,3,2,1,0:T(8,128)S(1)}, u32[]{:S(2)}, u32[]{:S(2)}) collective-permute-start(f32[2,2,2,32,256]{4,3,2,1,0:T(8,128)S(1)} %get-tuple-element.94), channel_id=1, source_target_pairs={{0,8},{2,10},{4,12},{6,14},{8,0},{10,2},{12,4},{14,6},{16,24},{18,... | collective-permute-start | bytes 786440 | tf_op jit(solution)/shard_map/ppermute | solution.py:265
  146.5 29.3 %collective-permute-start.13 = (f32[4,2,3,32,256]{4,3,2,1,0:T(8,128)S(1)}, f32[4,2,3,32,256]{4,3,2,1,0:T(8,128)S(1)}, u32[]{:S(2)}, u32[]{:S(2)}) collective-permute-start(f32[4,2,3,32,256]{4,3,2,1,0:T(8,128)S(1)} %get-tuple-element.95), channel_id=1, source_target_pairs={{0,4},{2,6},{4,0},{6,2},{8,12},{10,14},{12,8},{14,10},{16,20},{18,... | collective-permute-start | bytes 2359304 | tf_op jit(solution)/shard_map/ppermute | solution.py:265
  167.1 9.6 %collective-permute-start.14 = (f32[8,2,4,32,256]{4,3,2,1,0:T(8,128)S(1)}, f32[8,2,4,32,256]{4,3,2,1,0:T(8,128)S(1)}, u32[]{:S(2)}, u32[]{:S(2)}) collective-permute-start(f32[8,2,4,32,256]{4,3,2,1,0:T(8,128)S(1)} %get-tuple-element.97), channel_id=1, source_target_pairs={{0,2},{2,0},{4,6},{6,4},{8,10},{10,8},{12,14},{14,12},{16,18},{18,... | collective-permute-start | bytes 6291464 | tf_op jit(solution)/shard_map/ppermute | solution.py:265
  168.5 7.2 %copy-start.5 = (f32[2,2,2,32,256]{4,3,2,1,0:T(8,128)S(1)}, f32[2,2,2,32,256]{4,3,2,1,0:T(8,128)}, u32[]{:S(2)}) copy-start(f32[2,2,2,32,256]{4,3,2,1,0:T(8,128)} %get-tuple-element.169) | copy-start | bytes 786436
  178.1 27.8 %collective-permute-start.16 = (f32[1,2,2,32,256]{4,3,2,1,0:T(8,128)S(1)}, f32[1,2,2,32,256]{4,3,2,1,0:T(8,128)S(1)}, u32[]{:S(2)}, u32[]{:S(2)}) collective-permute-start(f32[1,2,2,32,256]{4,3,2,1,0:T(8,128)S(1)} %get-tuple-element.100), channel_id=1, source_target_pairs={{0,16},{2,18},{4,20},{6,22},{8,24},{10,26},{12,28},{14,30},{16,0},... | collective-permute-start | bytes 393224 | tf_op jit(solution)/shard_map/ppermute | solution.py:265
  181.3 24.7 %collective-permute-start.17 = (f32[2,2,3,32,256]{4,3,2,1,0:T(8,128)}, f32[2,2,3,32,256]{4,3,2,1,0:T(8,128)S(1)}, u32[]{:S(2)}, u32[]{:S(2)}) collective-permute-start(f32[2,2,3,32,256]{4,3,2,1,0:T(8,128)} %get-tuple-element.101), channel_id=1, source_target_pairs={{0,8},{2,10},{4,12},{6,14},{8,0},{10,2},{12,4},{14,6},{16,24},{18,... | collective-permute-start | bytes 1179656 | tf_op jit(solution)/shard_map/ppermute | solution.py:265
  182.9 25.2 %collective-permute-start.18 = (f32[4,2,4,32,256]{4,3,2,1,0:T(8,128)}, f32[4,2,4,32,256]{4,3,2,1,0:T(8,128)S(1)}, u32[]{:S(2)}, u32[]{:S(2)}) collective-permute-start(f32[4,2,4,32,256]{4,3,2,1,0:T(8,128)} %get-tuple-element.102), channel_id=1, source_target_pairs={{0,4},{2,6},{4,0},{6,2},{8,12},{10,14},{12,8},{14,10},{16,20},{18,... | collective-permute-start | bytes 3145736 | tf_op jit(solution)/shard_map/ppermute | solution.py:265
  189.4 18.8 %collective-permute-start.19 = (f32[8,2,5,32,256]{4,3,2,1,0:T(8,128)S(1)}, f32[8,2,5,32,256]{4,3,2,1,0:T(8,128)S(1)}, u32[]{:S(2)}, u32[]{:S(2)}) collective-permute-start(f32[8,2,5,32,256]{4,3,2,1,0:T(8,128)S(1)} %get-tuple-element.104), channel_id=1, source_target_pairs={{0,2},{2,0},{4,6},{6,4},{8,10},{10,8},{12,14},{14,12},{16,18},{18,... | collective-permute-start | bytes 7864328 | tf_op jit(solution)/shard_map/ppermute | solution.py:265
  209.0 9.0 %copy-start.14 = (f32[1,1,32,256]{3,2,1,0:T(8,128)S(1)}, f32[1,1,32,256]{3,2,1,0:T(8,128)}, u32[]{:S(2)}) copy-start(f32[1,1,32,256]{3,2,1,0:T(8,128)} %fusion.20) | copy-start | bytes 98308
  209.1 13.6 %copy-start.9 = (f32[1,2,1,32,256]{4,3,2,1,0:T(8,128)S(1)}, f32[1,2,1,32,256]{4,3,2,1,0:T(8,128)}, u32[]{:S(2)}) copy-start(f32[1,2,1,32,256]{4,3,2,1,0:T(8,128)} %get-tuple-element.183) | copy-start | bytes 196612
  209.1 13.6 %copy-start.13 = (f32[1,2,1,32,256]{4,3,2,1,0:T(8,128)S(1)}, f32[1,2,1,32,256]{4,3,2,1,0:T(8,128)}, u32[]{:S(2)}) copy-start(f32[1,2,1,32,256]{4,3,2,1,0:T(8,128)} %copy-done.12) | copy-start | bytes 196612
  209.1 16.5 %copy-start.11 = (f32[1,2,2,32,256]{4,3,2,1,0:T(8,128)S(1)}, f32[1,2,2,32,256]{4,3,2,1,0:T(8,128)}, u32[]{:S(2)}) copy-start(f32[1,2,2,32,256]{4,3,2,1,0:T(8,128)} %copy-done.10) | copy-start | bytes 393220
  209.1 30.2 %collective-permute-start.26 = (f32[4,2,5,32,256]{4,3,2,1,0:T(8,128)S(1)}, f32[4,2,5,32,256]{4,3,2,1,0:T(8,128)S(1)}, u32[]{:S(2)}, u32[]{:S(2)}) collective-permute-start(f32[4,2,5,32,256]{4,3,2,1,0:T(8,128)S(1)} %get-tuple-element.114), channel_id=1, source_target_pairs={{0,4},{2,6},{4,0},{6,2},{8,12},{10,14},{12,8},{14,10},{16,20},{18,... | collective-permute-start | bytes 3932168 | tf_op jit(solution)/shard_map/ppermute | solution.py:265
  217.5 22.1 %collective-permute-start.20 = (f32[8,2,3,32,256]{4,3,2,1,0:T(8,128)S(1)}, f32[8,2,3,32,256]{4,3,2,1,0:T(8,128)S(1)}, u32[]{:S(2)}, u32[]{:S(2)}) collective-permute-start(f32[8,2,3,32,256]{4,3,2,1,0:T(8,128)S(1)} %get-tuple-element.107), channel_id=1, source_target_pairs={{0,2},{2,0},{4,6},{6,4},{8,10},{10,8},{12,14},{14,12},{16,18},{18,... | collective-permute-start | bytes 4718600 | tf_op jit(solution)/shard_map/ppermute | solution.py:265
  217.5 22.4 %collective-permute-start.21 = (f32[8,2,3,32,256]{4,3,2,1,0:T(8,128)S(1)}, f32[8,2,3,32,256]{4,3,2,1,0:T(8,128)S(1)}, u32[]{:S(2)}, u32[]{:S(2)}) collective-permute-start(f32[8,2,3,32,256]{4,3,2,1,0:T(8,128)S(1)} %get-tuple-element.109), channel_id=1, source_target_pairs={{0,2},{2,0},{4,6},{6,4},{8,10},{10,8},{12,14},{14,12},{16,18},{18,... | collective-permute-start | bytes 4718600 | tf_op jit(solution)/shard_map/ppermute | solution.py:265
  218.0 3.9 %collective-permute-start.22 = (f32[1,1,32,256]{3,2,1,0:T(8,128)S(1)}, f32[1,1,32,256]{3,2,1,0:T(8,128)S(1)}, u32[]{:S(2)}, u32[]{:S(2)}) collective-permute-start(f32[1,1,32,256]{3,2,1,0:T(8,128)S(1)} %copy-done.14), channel_id=1, source_target_pairs={{0,1},{1,0},{2,3},{3,2},{4,5},{5,4},{6,7},{7,6},{8,9},{9,8},{10,11... | collective-permute-start | bytes 98312 | tf_op jit(solution)/shard_map/ppermute | solution.py:278
  219.6 4.3 %collective-permute-start.23 = (f32[1,2,32,256]{3,2,1,0:T(8,128)S(1)}, f32[1,2,32,256]{3,2,1,0:T(8,128)S(1)}, u32[]{:S(2)}, u32[]{:S(2)}) collective-permute-start(f32[1,2,32,256]{3,2,1,0:T(8,128)S(1)} %fusion.17), channel_id=1, source_target_pairs={{0,1},{1,0},{2,3},{3,2},{4,5},{5,4},{6,7},{7,6},{8,9},{9,8},{10,11... | collective-permute-start | bytes 196616 | tf_op jit(solution)/shard_map/ppermute | solution.py:278
  222.0 17.3 %collective-permute-start.25 = (f32[2,2,4,32,256]{4,3,2,1,0:T(8,128)S(1)}, f32[2,2,4,32,256]{4,3,2,1,0:T(8,128)S(1)}, u32[]{:S(2)}, u32[]{:S(2)}) collective-permute-start(f32[2,2,4,32,256]{4,3,2,1,0:T(8,128)S(1)} %get-tuple-element.113), channel_id=1, source_target_pairs={{0,8},{2,10},{4,12},{6,14},{8,0},{10,2},{12,4},{14,6},{16,24},{18,... | collective-permute-start | bytes 1572872 | tf_op jit(solution)/shard_map/ppermute | solution.py:265
  223.8 13.6 %collective-permute-start.24 = (f32[1,2,3,32,256]{4,3,2,1,0:T(8,128)S(1)}, f32[1,2,3,32,256]{4,3,2,1,0:T(8,128)S(1)}, u32[]{:S(2)}, u32[]{:S(2)}) collective-permute-start(f32[1,2,3,32,256]{4,3,2,1,0:T(8,128)S(1)} %get-tuple-element.112), channel_id=1, source_target_pairs={{0,16},{2,18},{4,20},{6,22},{8,24},{10,26},{12,28},{14,30},{16,0},... | collective-permute-start | bytes 589832 | tf_op jit(solution)/shard_map/ppermute | solution.py:265
  240.3 20.6 %collective-permute-start.31 = (f32[2,2,5,32,256]{4,3,2,1,0:T(8,128)S(1)}, f32[2,2,5,32,256]{4,3,2,1,0:T(8,128)S(1)}, u32[]{:S(2)}, u32[]{:S(2)}) collective-permute-start(f32[2,2,5,32,256]{4,3,2,1,0:T(8,128)S(1)} %get-tuple-element.121), channel_id=1, source_target_pairs={{0,8},{2,10},{4,12},{6,14},{8,0},{10,2},{12,4},{14,6},{16,24},{18,... | collective-permute-start | bytes 1966088 | tf_op jit(solution)/shard_map/ppermute | solution.py:265
  242.1 5.1 %collective-permute-start.29 = (f32[1,3,32,256]{3,2,1,0:T(8,128)S(1)}, f32[1,3,32,256]{3,2,1,0:T(8,128)S(1)}, u32[]{:S(2)}, u32[]{:S(2)}) collective-permute-start(f32[1,3,32,256]{3,2,1,0:T(8,128)S(1)} %fusion.14), channel_id=1, source_target_pairs={{0,1},{1,0},{2,3},{3,2},{4,5},{5,4},{6,7},{7,6},{8,9},{9,8},{10,11... | collective-permute-start | bytes 294920 | tf_op jit(solution)/shard_map/ppermute | solution.py:278
  243.7 20.5 %collective-permute-start.27 = (f32[4,2,3,32,256]{4,3,2,1,0:T(8,128)S(1)}, f32[4,2,3,32,256]{4,3,2,1,0:T(8,128)S(1)}, u32[]{:S(2)}, u32[]{:S(2)}) collective-permute-start(f32[4,2,3,32,256]{4,3,2,1,0:T(8,128)S(1)} %get-tuple-element.115), channel_id=1, source_target_pairs={{0,4},{2,6},{4,0},{6,2},{8,12},{10,14},{12,8},{14,10},{16,20},{18,... | collective-permute-start | bytes 2359304 | tf_op jit(solution)/shard_map/ppermute | solution.py:265
  244.2 16.0 %collective-permute-start.30 = (f32[1,2,4,32,256]{4,3,2,1,0:T(8,128)S(1)}, f32[1,2,4,32,256]{4,3,2,1,0:T(8,128)S(1)}, u32[]{:S(2)}, u32[]{:S(2)}) collective-permute-start(f32[1,2,4,32,256]{4,3,2,1,0:T(8,128)S(1)} %get-tuple-element.120), channel_id=1, source_target_pairs={{0,16},{2,18},{4,20},{6,22},{8,24},{10,26},{12,28},{14,30},{16,0},... | collective-permute-start | bytes 786440 | tf_op jit(solution)/shard_map/ppermute | solution.py:265
  246.2 31.3 %collective-permute-start.28 = (f32[4,2,3,32,256]{4,3,2,1,0:T(8,128)S(1)}, f32[4,2,3,32,256]{4,3,2,1,0:T(8,128)S(1)}, u32[]{:S(2)}, u32[]{:S(2)}) collective-permute-start(f32[4,2,3,32,256]{4,3,2,1,0:T(8,128)S(1)} %get-tuple-element.116), channel_id=1, source_target_pairs={{0,4},{2,6},{4,0},{6,2},{8,12},{10,14},{12,8},{14,10},{16,20},{18,... | collective-permute-start | bytes 2359304 | tf_op jit(solution)/shard_map/ppermute | solution.py:265
  277.6 5.0 %collective-permute-start.34 = (f32[1,4,32,256]{3,2,1,0:T(8,128)S(1)}, f32[1,4,32,256]{3,2,1,0:T(8,128)S(1)}, u32[]{:S(2)}, u32[]{:S(2)}) collective-permute-start(f32[1,4,32,256]{3,2,1,0:T(8,128)S(1)} %fusion.5), channel_id=1, source_target_pairs={{0,1},{1,0},{2,3},{3,2},{4,5},{5,4},{6,7},{7,6},{8,9},{9,8},{10,11... | collective-permute-start | bytes 393224 | tf_op jit(solution)/shard_map/ppermute | solution.py:278
  278.3 14.0 %collective-permute-start.35 = (f32[1,2,5,32,256]{4,3,2,1,0:T(8,128)S(1)}, f32[1,2,5,32,256]{4,3,2,1,0:T(8,128)S(1)}, u32[]{:S(2)}, u32[]{:S(2)}) collective-permute-start(f32[1,2,5,32,256]{4,3,2,1,0:T(8,128)S(1)} %get-tuple-element.128), channel_id=1, source_target_pairs={{0,16},{2,18},{4,20},{6,22},{8,24},{10,26},{12,28},{14,30},{16,0},... | collective-permute-start | bytes 983048 | tf_op jit(solution)/shard_map/ppermute | solution.py:265
  279.9 17.8 %collective-permute-start.32 = (f32[2,2,3,32,256]{4,3,2,1,0:T(8,128)S(1)}, f32[2,2,3,32,256]{4,3,2,1,0:T(8,128)S(1)}, u32[]{:S(2)}, u32[]{:S(2)}) collective-permute-start(f32[2,2,3,32,256]{4,3,2,1,0:T(8,128)S(1)} %get-tuple-element.122), channel_id=1, source_target_pairs={{0,8},{2,10},{4,12},{6,14},{8,0},{10,2},{12,4},{14,6},{16,24},{18,... | collective-permute-start | bytes 1179656 | tf_op jit(solution)/shard_map/ppermute | solution.py:265
  280.3 22.3 %collective-permute-start.33 = (f32[2,2,3,32,256]{4,3,2,1,0:T(8,128)S(1)}, f32[2,2,3,32,256]{4,3,2,1,0:T(8,128)S(1)}, u32[]{:S(2)}, u32[]{:S(2)}) collective-permute-start(f32[2,2,3,32,256]{4,3,2,1,0:T(8,128)S(1)} %get-tuple-element.123), channel_id=1, source_target_pairs={{0,8},{2,10},{4,12},{6,14},{8,0},{10,2},{12,4},{14,6},{16,24},{18,... | collective-permute-start | bytes 1179656 | tf_op jit(solution)/shard_map/ppermute | solution.py:265
  302.6 5.4 %collective-permute-start.38 = (f32[1,5,32,256]{3,2,1,0:T(8,128)S(1)}, f32[1,5,32,256]{3,2,1,0:T(8,128)S(1)}, u32[]{:S(2)}, u32[]{:S(2)}) collective-permute-start(f32[1,5,32,256]{3,2,1,0:T(8,128)S(1)} %fusion.2), channel_id=1, source_target_pairs={{0,1},{1,0},{2,3},{3,2},{4,5},{5,4},{6,7},{7,6},{8,9},{9,8},{10,11... | collective-permute-start | bytes 491528 | tf_op jit(solution)/shard_map/ppermute | solution.py:278
  304.0 13.0 %collective-permute-start.36 = (f32[1,2,3,32,256]{4,3,2,1,0:T(8,128)S(1)}, f32[1,2,3,32,256]{4,3,2,1,0:T(8,128)S(1)}, u32[]{:S(2)}, u32[]{:S(2)}) collective-permute-start(f32[1,2,3,32,256]{4,3,2,1,0:T(8,128)S(1)} %get-tuple-element.129), channel_id=1, source_target_pairs={{0,16},{2,18},{4,20},{6,22},{8,24},{10,26},{12,28},{14,30},{16,0},... | collective-permute-start | bytes 589832 | tf_op jit(solution)/shard_map/ppermute | solution.py:265
  304.1 15.5 %collective-permute-start.37 = (f32[1,2,3,32,256]{4,3,2,1,0:T(8,128)S(1)}, f32[1,2,3,32,256]{4,3,2,1,0:T(8,128)S(1)}, u32[]{:S(2)}, u32[]{:S(2)}) collective-permute-start(f32[1,2,3,32,256]{4,3,2,1,0:T(8,128)S(1)} %get-tuple-element.130), channel_id=1, source_target_pairs={{0,16},{2,18},{4,20},{6,22},{8,24},{10,26},{12,28},{14,30},{16,0},... | collective-permute-start | bytes 589832 | tf_op jit(solution)/shard_map/ppermute | solution.py:265
  319.7 4.7 %collective-permute-start.39 = (f32[1,3,32,256]{3,2,1,0:T(8,128)S(1)}, f32[1,3,32,256]{3,2,1,0:T(8,128)S(1)}, u32[]{:S(2)}, u32[]{:S(2)}) collective-permute-start(f32[1,3,32,256]{3,2,1,0:T(8,128)S(1)} %fusion.11), channel_id=1, source_target_pairs={{0,1},{1,0},{2,3},{3,2},{4,5},{5,4},{6,7},{7,6},{8,9},{9,8},{10,11... | collective-permute-start | bytes 294920 | tf_op jit(solution)/shard_map/ppermute | solution.py:278
  320.4 5.0 %collective-permute-start.40 = (f32[1,3,32,256]{3,2,1,0:T(8,128)S(1)}, f32[1,3,32,256]{3,2,1,0:T(8,128)S(1)}, u32[]{:S(2)}, u32[]{:S(2)}) collective-permute-start(f32[1,3,32,256]{3,2,1,0:T(8,128)S(1)} %fusion.10), channel_id=1, source_target_pairs={{0,1},{1,0},{2,3},{3,2},{4,5},{5,4},{6,7},{7,6},{8,9},{9,8},{10,11... | collective-permute-start | bytes 294920 | tf_op jit(solution)/shard_map/ppermute | solution.py:278
  (9 other events, 24.5 us)
